TPU v7x, 32 devices: a whole 2x2x4 slice. The times are simulated.
32 devices in a mesh: dp: 8 (over z, y), mp: 4 (over x, core).
Axes of the slice: x: 2, y: 2, z: 4, core: 2. Of those that a mesh axis runs over, the one named last changes fastest.
Arguments:
- tokens: bfloat16 [24576, 768], P('dp'), may hold values from -6 to 6
- seg_ids: int32 [24576], P('dp'), may hold values from 0 to 180, as said below
- labels: int32 [1440], P('dp'), may hold values from 0 to 999
- w_qkv: float32 [3, 768, 768], P(None, 'dp', 'mp'), may hold values from -0.21875 to 0.21875
- m_qkv: float32 [3, 768, 768], P(None, 'dp', 'mp'), may hold values from -0.0009765625 to 0.0009765625
- v_qkv: float32 [3, 768, 768], P(None, 'dp', 'mp'), may hold values from 1.890432e-09 to 7.561728e-09
- w_out: float32 [768, 768], P('mp', 'dp'), may hold values from -0.4375 to 0.4375
- m_out: float32 [768, 768], P('mp', 'dp'), may hold values from -0.0009765625 to 0.0009765625
- v_out: float32 [768, 768], P('mp', 'dp'), may hold values from 1.890432e-09 to 7.561728e-09
- w_up: float32 [768, 3072], P('dp', 'mp'), may hold values from -0.21875 to 0.21875
- m_up: float32 [768, 3072], P('dp', 'mp'), may hold values from -0.0004272461 to 0.0004272461
- v_up: float32 [768, 3072], P('dp', 'mp'), may hold values from 4.72608e-10 to 1.890432e-09
- w_down: float32 [3072, 768], P('mp', 'dp'), may hold values from -0.109375 to 0.109375
- m_down: float32 [3072, 768], P('mp', 'dp'), may hold values from -0.0004272461 to 0.0004272461
- v_down: float32 [3072, 768], P('mp', 'dp'), may hold values from 4.72608e-10 to 1.890432e-09
- w_cls: float32 [768, 1000], P('dp', 'mp')
- m_cls: float32 [768, 1000], P('dp', 'mp'), may hold values from -0.00030517578 to 0.00030517578
- v_cls: float32 [768, 1000], P('dp', 'mp'), may hold values from 2.5e-10 to 1e-09
- norm_params: float32 [7, 768], P(None, 'dp')
- m_norm: float32 [7, 768], P(None, 'dp'), may hold values from -0.0009765625 to 0.0009765625
- v_norm: float32 [7, 768], P(None, 'dp'), may hold values from 1.890432e-09 to 7.561728e-09
- qk_gain: float32 [2, 12, 64], P(None, 'mp', 'dp'), may hold values from 1.2 to 1.6
- m_qk: float32 [2, 12, 64], P(None, 'mp', 'dp'), may hold values from -0.0009765625 to 0.0009765625
- v_qk: float32 [2, 12, 64], P(None, 'mp', 'dp'), may hold values from 1.890432e-09 to 7.561728e-09
Outputs:
- block_out: bfloat16 [24576, 768], P('dp')
- input_grad: float32 [24576, 768], P('dp')
- mean_loss: float32 [], replicated
- m_qkv_new: float32 [3, 768, 768], P(None, 'dp', 'mp')
- v_qkv_new: float32 [3, 768, 768], P(None, 'dp', 'mp')
- w_qkv_new: float32 [3, 768, 768], P(None, 'dp', 'mp')
- m_out_new: float32 [768, 768], P('mp', 'dp')
- v_out_new: float32 [768, 768], P('mp', 'dp')
- w_out_new: float32 [768, 768], P('mp', 'dp')
- m_up_new: float32 [768, 3072], P('dp', 'mp')
- v_up_new: float32 [768, 3072], P('dp', 'mp')
- w_up_new: float32 [768, 3072], P('dp', 'mp')
- m_down_new: float32 [3072, 768], P('mp', 'dp')
- v_down_new: float32 [3072, 768], P('mp', 'dp')
- w_down_new: float32 [3072, 768], P('mp', 'dp')
- m_cls_new: float32 [768, 1000], P('dp', 'mp')
- v_cls_new: float32 [768, 1000], P('dp', 'mp')
- w_cls_new: float32 [768, 1000], P('dp', 'mp')
- m_norm_new: float32 [7, 768], P(None, 'dp')
- v_norm_new: float32 [6, 768], P(None, 'dp')
- v_probe_new: float32 [768], P('dp')
- norm_new: float32 [7, 768], P(None, 'dp')
- m_qk_new: float32 [2, 12, 64], P(None, 'mp', 'dp')
- v_qk_new: float32 [2, 12, 64], P(None, 'mp', 'dp')
- qk_new: float32 [2, 12, 64], P(None, 'mp', 'dp')
Inputs may be any that keep to these rules, and one draw needn't show every extreme that they name: `seg_ids`: each of the 3 sequences of 1024 positions on a data device holds, from its start, images one after another numbered k * 60 + j for its number k on the device and j = 0, 1, ..., each of one position or more, at least 512 positions in all; the rest, one position or more at its end, holds 180.
All inputs are finite; a program needn't handle non-finite values.
Results may differ from a plain program's by a relative error of at most 0.017.
The roundings to bfloat16 on the way count: a program that leaves them out, or rounds other values in their place, can miss the bound.
Values may be sent and summed in bfloat16 or wider, within the bound.
A program may use at most 256 MiB of HBM per device.

v0:
```python
import jax
import jax.numpy as jnp
from jax import lax
from jax.sharding import PartitionSpec as P

LEN = 1024
STEP = 10
SEQ_DEV = 3
IMG_DEV = 180


NORM_EPS = 1e-06
MASK_FILL = -1000000000.0
BETA_ONE = 0.9
BETA_TWO = 0.999
ADAM_EPS = 1e-08
MATRIX_RATE = 0.1
MATRIX_DECAY = 0.1
GAIN_RATE = 0.8


def combined_all(value, axis, join):
    pieces = jax.tree.map(lambda part: lax.all_gather(part, axis), value)
    head = jax.tree.map(lambda part: part[0], pieces)
    tail = jax.tree.map(lambda part: part[1:], pieces)
    subtotal, _ = lax.scan(lambda subtotal, section: (join(subtotal, section), None), head, tail)
    return subtotal


def layer_norm(values, gain_row, shift_row):
    centre = values - jnp.mean(values, axis=-1, keepdims=True)
    spread = jnp.mean(centre * centre, axis=-1, keepdims=True)
    return centre * lax.rsqrt(spread + NORM_EPS) * gain_row + shift_row


def head_norm(values, gain_row):
    centre = values - jnp.mean(values, axis=-1, keepdims=True)
    spread = jnp.mean(centre * centre, axis=-1, keepdims=True)
    return centre * lax.rsqrt(spread + NORM_EPS) * gain_row


def exact_gelu(values):
    return jax.nn.gelu(values, approximate=False)


def pool_weights(normed, probe_row, image_ids, images):
    pool_score = jnp.dot(normed, probe_row, precision=lax.Precision.HIGHEST)
    member = image_ids[None, :] == jnp.arange(images, dtype=jnp.int32)[:, None]
    image_top = jnp.max(jnp.where(member, pool_score[None, :], MASK_FILL), axis=1)
    shifted = jnp.where(member, pool_score[None, :] - image_top[:, None], MASK_FILL)
    weight = jnp.exp(shifted)
    non_empty = jnp.any(member, axis=1)
    image_sum = jnp.sum(weight, axis=1) + jnp.where(non_empty, 0.0, 1.0)
    return weight / image_sum[:, None]


def attend(query_slot, key_slot, value_slot, seg_slot, score_scale):
    raw_scores = (
        jnp.einsum("qhe,khe->hqk", query_slot, key_slot, preferred_element_type=jnp.float32)
        * score_scale
    )
    same_image = seg_slot[:, None] == seg_slot[None, :]
    masked = jnp.where(same_image[None], raw_scores, MASK_FILL)
    row_top = jnp.max(masked, axis=-1, keepdims=True)
    exp_scores = jnp.exp(masked - row_top)
    row_total = jnp.sum(exp_scores, axis=-1, keepdims=True)
    soft_probs = (exp_scores / row_total).astype(jnp.bfloat16)
    slot_out = jnp.einsum(
        "hqk,khe->qhe", soft_probs, value_slot, preferred_element_type=jnp.float32
    )
    return (slot_out, row_top + jnp.log(row_total))


def attend_back(query_slot, key_slot, value_slot, grad_slot, seg_slot, log_slot, score_scale):
    raw_scores = (
        jnp.einsum("qhe,khe->hqk", query_slot, key_slot, preferred_element_type=jnp.float32)
        * score_scale
    )
    same_image = seg_slot[:, None] == seg_slot[None, :]
    masked = jnp.where(same_image[None], raw_scores, MASK_FILL)
    soft_probs = jnp.exp(masked - log_slot)
    prob_grad = jnp.einsum(
        "qhe,khe->hqk", grad_slot, value_slot, preferred_element_type=jnp.float32
    )
    inner = jnp.sum(soft_probs * prob_grad, axis=-1, keepdims=True)
    score_grad = (soft_probs * (prob_grad - inner)).astype(jnp.bfloat16)
    query_grad = (
        jnp.einsum("hqk,khe->qhe", score_grad, key_slot, preferred_element_type=jnp.float32)
        * score_scale
    )
    key_grad = (
        jnp.einsum("hqk,qhe->khe", score_grad, query_slot, preferred_element_type=jnp.float32)
        * score_scale
    )
    value_grad = jnp.einsum(
        "hqk,qhe->khe",
        soft_probs.astype(jnp.bfloat16),
        grad_slot,
        preferred_element_type=jnp.float32,
    )
    return (query_grad, key_grad, value_grad)


def adam_update(weight, moment_one, moment_two, gradient, step_rate, decay_rate):
    fresh_one = BETA_ONE * moment_one + (1.0 - BETA_ONE) * gradient
    fresh_two = BETA_TWO * moment_two + (1.0 - BETA_TWO) * gradient * gradient
    one_hat = fresh_one / (1.0 - BETA_ONE**STEP)
    two_hat = fresh_two / (1.0 - BETA_TWO**STEP)
    updated = weight - step_rate * (one_hat / (jnp.sqrt(two_hat) + ADAM_EPS) + decay_rate * weight)
    return (fresh_one, fresh_two, updated)


def shards(
    tokens,
    seg_ids,
    labels,
    w_qkv,
    m_qkv,
    v_qkv,
    w_out,
    m_out,
    v_out,
    w_up,
    m_up,
    v_up,
    w_down,
    m_down,
    v_down,
    w_cls,
    m_cls,
    v_cls,
    norm_params,
    m_norm,
    v_norm,
    qk_gain,
    m_qk,
    v_qk,
):
    gathered = (
        lax.all_gather(w_qkv.astype(jnp.bfloat16), "dp", axis=1, tiled=True),
        lax.all_gather(w_out.astype(jnp.bfloat16), "dp", axis=1, tiled=True),
        lax.all_gather(w_up.astype(jnp.bfloat16), "dp", axis=0, tiled=True),
        lax.all_gather(w_down.astype(jnp.bfloat16), "dp", axis=1, tiled=True),
        lax.all_gather(w_cls.astype(jnp.bfloat16), "dp", axis=0, tiled=True),
        lax.all_gather(norm_params.astype(jnp.bfloat16), "dp", axis=1, tiled=True),
        lax.all_gather(qk_gain.astype(jnp.bfloat16), "dp", axis=2, tiled=True),
    )
    qkv_full, out_full, up_full, down_full, cls_full, norm_full, qk_full = gathered
    params = norm_full.astype(jnp.float32)
    qk_scale = qk_full.astype(jnp.float32)
    inputs = tokens.astype(jnp.float32)
    row_count = tokens.shape[0]
    local_heads = qk_full.shape[1]
    head_dim = qk_full.shape[2]
    score_scale = head_dim ** (-0.5)
    normed_one, first_back = jax.vjp(layer_norm, inputs, params[0], params[1])
    normed_low = normed_one.astype(jnp.bfloat16)
    projected = jnp.einsum("rd,pde->pre", normed_low, qkv_full, preferred_element_type=jnp.float32)
    shaped = projected.reshape(3, row_count, local_heads, head_dim)
    query_norm, query_back = jax.vjp(head_norm, shaped[0], qk_scale[0])
    key_norm, key_back = jax.vjp(head_norm, shaped[1], qk_scale[1])
    query_low = query_norm.astype(jnp.bfloat16)
    key_low = key_norm.astype(jnp.bfloat16)
    value_low = shaped[2].astype(jnp.bfloat16)
    slot_shape = (SEQ_DEV, LEN, local_heads, head_dim)
    slot_seg = seg_ids.reshape(SEQ_DEV, LEN)
    slot_query = query_low.reshape(slot_shape)
    slot_key = key_low.reshape(slot_shape)
    slot_value = value_low.reshape(slot_shape)
    attended, log_totals = lax.map(
        lambda pieces: attend(pieces[0], pieces[1], pieces[2], pieces[3], score_scale),
        (slot_query, slot_key, slot_value, slot_seg),
    )
    attn_low = attended.reshape(row_count, local_heads * head_dim).astype(jnp.bfloat16)
    head_terms = jnp.dot(attn_low, out_full, preferred_element_type=jnp.float32)
    attn_sum = lax.psum(head_terms, "mp")
    middle = inputs + attn_sum
    normed_two, second_back = jax.vjp(layer_norm, middle, params[2], params[3])
    second_low = normed_two.astype(jnp.bfloat16)
    hidden = jnp.dot(second_low, up_full, preferred_element_type=jnp.float32)
    active_low = exact_gelu(hidden).astype(jnp.bfloat16)
    down_terms = jnp.dot(active_low, down_full, preferred_element_type=jnp.float32)
    mlp_sum = lax.psum(down_terms, "mp")
    result = middle + mlp_sum
    final_norm, final_back = jax.vjp(layer_norm, result, params[4], params[5])
    pool_share, pool_back = jax.vjp(
        lambda normed, probe_row: pool_weights(normed, probe_row, seg_ids, IMG_DEV),
        final_norm,
        params[6],
    )
    share_low = pool_share.astype(jnp.bfloat16)
    final_low = final_norm.astype(jnp.bfloat16)
    pooled = jnp.dot(share_low, final_low, preferred_element_type=jnp.float32)
    pooled_low = pooled.astype(jnp.bfloat16)
    logits = jnp.dot(pooled_low, cls_full, preferred_element_type=jnp.float32)
    class_count = cls_full.shape[1]
    first_class = lax.axis_index("mp") * class_count
    class_ids = first_class + jnp.arange(class_count, dtype=jnp.int32)
    chosen = (labels[:, None] == class_ids[None, :]).astype(jnp.float32)
    local_top = jnp.max(logits, axis=1)
    local_total = jnp.sum(jnp.exp(logits - local_top[:, None]), axis=1)
    local_label = jnp.sum(chosen * logits, axis=1)

    def combine(left_part, right_part):
        joint_top = jnp.maximum(left_part[0], right_part[0])
        joint_total = left_part[1] * jnp.exp(left_part[0] - joint_top) + right_part[1] * jnp.exp(
            right_part[0] - joint_top
        )
        return (joint_top, joint_total, left_part[2] + right_part[2])

    top_all, total_all, label_logit = combined_all(
        (local_top, local_total, local_label), "mp", combine
    )
    log_total = top_all + jnp.log(total_all)
    member_count = jnp.sum(
        (seg_ids[None, :] == jnp.arange(IMG_DEV, dtype=jnp.int32)[:, None]).astype(jnp.float32),
        axis=1,
    )
    present = jnp.where(member_count > 0, 1.0, 0.0).astype(jnp.float32)
    loss_terms = jnp.sum(present * (log_total - label_logit))
    loss_sum, image_total = lax.psum((loss_terms, jnp.sum(present)), "dp")
    mean_loss = loss_sum / image_total
    soft_class = jnp.exp(logits - log_total[:, None])
    logit_grad = ((soft_class - chosen) * (present / image_total)[:, None]).astype(jnp.bfloat16)
    grad_cls = jnp.einsum("id,ic->dc", pooled_low, logit_grad, preferred_element_type=jnp.float32)
    pool_terms = jnp.einsum("ic,dc->id", logit_grad, cls_full, preferred_element_type=jnp.float32)
    pooled_grad = lax.psum(pool_terms, "mp").astype(jnp.bfloat16)
    share_grad = jnp.einsum("id,td->it", pooled_grad, final_low, preferred_element_type=jnp.float32)
    final_grad = jnp.einsum("it,id->td", share_low, pooled_grad, preferred_element_type=jnp.float32)
    share_part, probe_grad = pool_back(share_grad)
    result_grad, final_gain, final_shift = final_back(final_grad + share_part)
    result_low = result_grad.astype(jnp.bfloat16)
    grad_down = jnp.einsum("rf,rd->fd", active_low, result_low, preferred_element_type=jnp.float32)
    active_grad = jnp.einsum("rd,fd->rf", result_low, down_full, preferred_element_type=jnp.float32)
    hidden_low = jax.vjp(exact_gelu, hidden)[1](active_grad)[0].astype(jnp.bfloat16)
    grad_up = jnp.einsum("rd,rf->df", second_low, hidden_low, preferred_element_type=jnp.float32)
    second_terms = jnp.einsum("rf,df->rd", hidden_low, up_full, preferred_element_type=jnp.float32)
    second_grad = lax.psum(second_terms.astype(jnp.bfloat16), "mp").astype(jnp.float32)
    middle_part, gain_two, shift_two = second_back(second_grad)
    middle_grad = result_grad + middle_part
    middle_low = middle_grad.astype(jnp.bfloat16)
    grad_out = jnp.einsum("rc,rd->cd", attn_low, middle_low, preferred_element_type=jnp.float32)
    attn_grad = jnp.einsum(
        "rd,cd->rc", middle_low, out_full, preferred_element_type=jnp.float32
    ).astype(jnp.bfloat16)
    slot_grad = attn_grad.reshape(slot_shape)
    query_part, key_part, value_part = lax.map(
        lambda pieces: attend_back(
            pieces[0], pieces[1], pieces[2], pieces[3], pieces[4], pieces[5], score_scale
        ),
        (slot_query, slot_key, slot_value, slot_grad, slot_seg, log_totals),
    )
    head_shape = (row_count, local_heads, head_dim)
    query_grad, query_gain = query_back(query_part.reshape(head_shape))
    key_grad, key_gain = key_back(key_part.reshape(head_shape))
    proj_grad = (
        jnp.stack([query_grad, key_grad, value_part.reshape(head_shape)])
        .reshape(3, row_count, local_heads * head_dim)
        .astype(jnp.bfloat16)
    )
    grad_qkv = jnp.einsum("rd,pre->pde", normed_low, proj_grad, preferred_element_type=jnp.float32)
    first_terms = jnp.einsum("pre,pde->rd", proj_grad, qkv_full, preferred_element_type=jnp.float32)
    first_grad = lax.psum(first_terms.astype(jnp.bfloat16), "mp").astype(jnp.float32)
    input_part, gain_one, shift_one = first_back(first_grad)
    input_grad = middle_grad + input_part
    norm_grads = jnp.stack(
        [gain_one, shift_one, gain_two, shift_two, final_gain, final_shift, probe_grad]
    )
    qk_grads = jnp.stack([query_gain, key_gain])
    reduced = (
        lax.psum_scatter(grad_qkv, "dp", scatter_dimension=1, tiled=True),
        lax.psum_scatter(grad_out, "dp", scatter_dimension=1, tiled=True),
        lax.psum_scatter(grad_up, "dp", scatter_dimension=0, tiled=True),
        lax.psum_scatter(grad_down, "dp", scatter_dimension=1, tiled=True),
        lax.psum_scatter(grad_cls, "dp", scatter_dimension=0, tiled=True),
        lax.psum_scatter(norm_grads, "dp", scatter_dimension=1, tiled=True),
        lax.psum_scatter(qk_grads, "dp", scatter_dimension=2, tiled=True),
    )
    groups = (
        (w_qkv, m_qkv, v_qkv, MATRIX_RATE, MATRIX_DECAY),
        (w_out, m_out, v_out, MATRIX_RATE, MATRIX_DECAY),
        (w_up, m_up, v_up, MATRIX_RATE, MATRIX_DECAY),
        (w_down, m_down, v_down, MATRIX_RATE, MATRIX_DECAY),
        (w_cls, m_cls, v_cls, MATRIX_RATE, MATRIX_DECAY),
        (norm_params, m_norm, v_norm, GAIN_RATE, 0.0),
        (qk_gain, m_qk, v_qk, GAIN_RATE, 0.0),
    )
    outputs = [result.astype(jnp.bfloat16), input_grad, mean_loss]
    for number, group in enumerate(groups):
        fresh_one, fresh_two, updated = adam_update(
            group[0], group[1], group[2], reduced[number], group[3], group[4]
        )
        if number == 5:
            outputs = outputs + [fresh_one, fresh_two[:6], fresh_two[6], updated]
        else:
            outputs = outputs + [fresh_one, fresh_two, updated]
    return tuple(outputs)


def solution(mesh):
    in_specs = (
        P("dp", None),
        P("dp"),
        P("dp"),
        P(None, "dp", "mp"),
        P(None, "dp", "mp"),
        P(None, "dp", "mp"),
        P("mp", "dp"),
        P("mp", "dp"),
        P("mp", "dp"),
        P("dp", "mp"),
        P("dp", "mp"),
        P("dp", "mp"),
        P("mp", "dp"),
        P("mp", "dp"),
        P("mp", "dp"),
        P("dp", "mp"),
        P("dp", "mp"),
        P("dp", "mp"),
        P(None, "dp"),
        P(None, "dp"),
        P(None, "dp"),
        P(None, "mp", "dp"),
        P(None, "mp", "dp"),
        P(None, "mp", "dp"),
    )
    out_specs = (
        P("dp", None),
        P("dp", None),
        P(),
        P(None, "dp", "mp"),
        P(None, "dp", "mp"),
        P(None, "dp", "mp"),
        P("mp", "dp"),
        P("mp", "dp"),
        P("mp", "dp"),
        P("dp", "mp"),
        P("dp", "mp"),
        P("dp", "mp"),
        P("mp", "dp"),
        P("mp", "dp"),
        P("mp", "dp"),
        P("dp", "mp"),
        P("dp", "mp"),
        P("dp", "mp"),
        P(None, "dp"),
        P(None, "dp"),
        P("dp"),
        P(None, "dp"),
        P(None, "mp", "dp"),
        P(None, "mp", "dp"),
        P(None, "mp", "dp"),
    )
    return jax.shard_map(shards, mesh=mesh, in_specs=in_specs, out_specs=out_specs, check_vma=False)
```

profile of v0, /device:TPU:0, one launch (start us, length us, event | category | flops | bytes accessed | tf_op | source)
XLA Modules:
  0.0 1566.3 jit_solution(11296908697479802045)
XLA Ops:
  8.8 27.8 %all-gather.3 = bf16[8,96,7]{1,2,0:T(8,128)(2,1)S(1)} all-gather(bf16[1,96,7]{1,2,0:T(8,128)(2,1)S(1)} %convert_bitcast_fusion), channel_id=1, replica_groups=mesh['dp'=8,'mp'=4] {'dp'}, dimensions={0}, use_global_device_ids=true | all-gather | bytes 12096 | tf_op jit(solution)/shard_map/all_gather | solution.py:145
  44.0 35.3 %all_gather.40 = bf16[3,768,192]{2,0,1:T(4,128)(2,1)S(1)} all-gather(bf16[3,96,192]{2,0,1:T(4,128)(2,1)S(1)} %copy.158), channel_id=1, replica_groups=mesh['dp'=8,'mp'=4] {'dp'}, dimensions={1}, use_global_device_ids=true | all-gather | bytes 995328 | tf_op jit(solution)/shard_map/all_gather | solution.py:140
  106.4 30.6 %all_gather.41 = bf16[2,3,64]{1,0,2:T(2,128)(2,1)S(1)} all-gather(bf16[2,3,8]{1,0,2:T(2,128)(2,1)S(1)} %copy.160), channel_id=1, replica_groups=mesh['dp'=8,'mp'=4] {'dp'}, dimensions={2}, use_global_device_ids=true | all-gather | bytes 864 | tf_op jit(solution)/shard_map/all_gather | solution.py:146
  148.6 45.3 %while.40 = (s32[]{:T(128)}, bf16[3,1024,3,64]{1,3,2,0:T(8,128)(2,1)}, f32[3,3,1024,1]{2,1,3,0:T(4,128)}, bf16[3,1024,3,64]{1,3,2,0:T(8,128)(2,1)}, s32[3,1024]{...) while((s32[]{:T(128)}, ...), condition=%wide.region_9.10_spmd, body=%wide.region_6.9_spmd.sunk | while | flops 844100608 | bytes 48220788 | solution.py:170
  197.0 31.4 %all_gather.42 = bf16[192,768]{0,1:T(8,128)(2,1)S(1)} all-gather(bf16[192,96]{0,1:T(8,128)(2,1)S(1)} %copy.167), channel_id=1, replica_groups=mesh['dp'=8,'mp'=4] {'dp'}, dimensions={1}, use_global_device_ids=true | all-gather | bytes 331776 | tf_op jit(solution)/shard_map/all_gather | solution.py:141
  236.9 167.0 %all-reduce.12.cloned.1.call-done = f32[3072,768]{1,0:T(8,128)} async-done(((f32[3072,768]{1,0:T(8,128)}), f32[3072,768]{1,0:T(8,128)}) %all-reduce.12.cloned.1.call-update) | async-done | bytes 9437200 | tf_op jit(solution)/shard_map/psum | solution.py:176
  403.8 9.7 fusion.156
  423.3 26.3 %multiply_convert_fusion.1 = (bf16[3072,768]{1,0:T(8,128)(2,1)}, f32[3072,768]{1,0:T(8,128)}, f32[3072,768]{1,0:T(8,128)}) fusion(bf16[3072,768]{1,0:T(8,128)(2,1)} %add_convert_fusion.1, bf16[768,768]{1,0:T(8,128)(2,1)} %all-gather.7.cloned.1.call-done), kind=kOutput, calls=%fused_computation.102 | convolution fusion | flops 3777232896 | bytes 29491200 | tf_op jit(solution)/shard_map/dot_general | solution.py:180
  449.7 10.1 fusion.161
  462.4 31.3 %all_gather.45 = bf16[768,250]{1,0:T(8,128)(2,1)S(1)} all-gather(bf16[96,250]{1,0:T(8,128)(2,1)S(1)} %convert_element_type.140), channel_id=1, replica_groups=mesh['dp'=8,'mp'=4] {'dp'}, dimensions={0}, use_global_device_ids=true | all-gather | bytes 432000 | tf_op jit(solution)/shard_map/all_gather | solution.py:144
  493.7 136.3 %all-reduce.14.cloned.1.call-done = f32[3072,768]{1,0:T(8,128)} async-done(((f32[3072,768]{1,0:T(8,128)}), f32[3072,768]{1,0:T(8,128)}) %all-reduce.14.cloned.1.call-update) | async-done | bytes 9437200 | tf_op jit(solution)/shard_map/psum | solution.py:183
  630.0 10.9 fusion.154
  648.9 6.5 fusion.76
  660.3 10.1 all-reduce.5
  671.7 22.2 %psum.51 = f32[]{:T(128)} all-reduce(f32[]{:T(128)} %get-tuple-element.362), channel_id=1, replica_groups=mesh['dp'=8,'mp'=4] {'dp'}, use_global_device_ids=true, to_apply=%region_26.27 | all-reduce | flops 1 | bytes 8 | tf_op jit(solution)/shard_map/psum | solution.py:221
  695.4 16.5 %all-reduce.19 = bf16[180,768]{1,0:T(8,128)(2,1)S(1)} all-reduce(f32[180,768]{1,0:T(8,128)S(1)} %fusion.136), channel_id=1, replica_groups=mesh['dp'=8,'mp'=4] {'mp'}, use_global_device_ids=true, to_apply=%region_27.28 | all-reduce | flops 138240 | bytes 829440 | tf_op jit(solution)/shard_map/psum | solution.py:227
  723.7 7.1 fusion.153
  730.8 15.1 add_convert_fusion
  755.1 89.5 %all-reduce.16.cloned.1.call-done = bf16[3072,768]{1,0:T(8,128)(2,1)} async-done(((bf16[3072,768]{1,0:T(8,128)(2,1)}), bf16[3072,768]{1,0:T(8,128)(2,1)}) %all-reduce.16.cloned.1.call-update) | async-done | bytes 4718608 | tf_op jit(solution)/shard_map/psum | solution.py:238
  844.6 8.4 convert_reduce_fusion.1
  853.0 7.7 fusion.65
  860.8 7.7 add_add_fusion.4
  878.4 209.7 %while.42 = (s32[]{:T(128)}, f32[3,1024,3,64]{1,0,3,2:T(4,128)}, f32[3,1024,3,64]{1,0,3,2:T(4,128)}, bf16[3,1024,3,64]{1,3,2,0:T(8,128)(2,1)}, bf16[3,1024,3,64]...) while((s32[]{:T(128)}, f32[3,1024,3,64]{1,0,3,2:T(4,128)}, ...), condition=%wide.region_40.41_spmd, body=%wide.region_38.40_spmd.sunk | while | flops 2061890560 | bytes 164597936 | solution.py:247
  903.8 15.3 dynamic_update_slice.29
  924.1 15.3 dynamic_update_slice.28
  939.4 8.9 fusion.221
  955.0 6.4 multiply_reduce_fusion.14
  973.6 15.3 dynamic_update_slice.29
  993.9 15.3 dynamic_update_slice.28
  1009.2 8.9 fusion.221
  1024.7 6.4 multiply_reduce_fusion.14
  1043.4 15.3 dynamic_update_slice.29
  1063.7 15.3 dynamic_update_slice.28
  1079.0 8.9 fusion.221
  1117.9 8.8 multiply_reduce_fusion.5
  1147.0 6.6 fusion.101
  1153.6 10.7 fusion.138
  1164.5 9.3 fusion.162
  1175.3 8.9 fusion.74
  1185.3 54.1 %all-reduce.18.cloned.1.call-done = bf16[3072,768]{1,0:T(8,128)(2,1)} async-done(((bf16[3072,768]{1,0:T(8,128)(2,1)}), bf16[3072,768]{1,0:T(8,128)(2,1)}) %all-reduce.18.cloned.1.call-update) | async-done | bytes 4718608 | tf_op jit(solution)/shard_map/psum | solution.py:263
  1246.6 7.8 fusion.66
  1258.8 6.8 fusion.98
  1278.4 22.6 %all-reduce.4 = (f32[]{:T(128)}, f32[2,3,64]{2,1,0:T(4,128)S(1)}) all-reduce(f32[]{:T(128)} %get-tuple-element.361, f32[2,3,64]{2,1,0:T(4,128)S(1)} %pad_maximum_fusion.3), channel_id=1, replica_groups=mesh['dp'=8,'mp'=4] {'dp'}, use_global_device_ids=true, to_apply=%region_49.50 | all-reduce | flops 385 | bytes 3080 | tf_op jit(solution)/shard_map/psum | solution.py:221
  1308.3 40.2 %reduce-scatter.16.cloned.1.call-done = f32[768,96]{0,1:T(8,128)} async-done(((f32[768,768]{0,1:T(8,128)}), f32[768,96]{0,1:T(8,128)}) %reduce-scatter.16.cloned.1.call-update) | async-done | bytes 294928 | tf_op jit(solution)/shard_map/reduce_scatter | solution.py:274
  1350.8 69.6 %reduce-scatter.14.cloned.1.call-done = f32[96,768]{1,0:T(8,128)} async-done(((f32[768,768]{1,0:T(8,128)}), f32[96,768]{1,0:T(8,128)}) %reduce-scatter.14.cloned.1.call-update) | async-done | bytes 294928 | tf_op jit(solution)/shard_map/reduce_scatter | solution.py:273
  1422.5 12.0 add_add_fusion.3
  1434.5 49.7 %reduce-scatter.24.cloned.1.call-done = f32[96,7]{1,0:T(8,128)} async-done(((f32[768,7]{1,0:T(8,128)}), f32[96,7]{1,0:T(8,128)}) %reduce-scatter.24.cloned.1.call-update) | async-done | bytes 2704
  1486.2 67.4 %reduce-scatter.20.cloned.1.call-done = f32[96,576]{1,0:T(8,128)} async-done(((f32[768,576]{1,0:T(8,128)}), f32[96,576]{1,0:T(8,128)}) %reduce-scatter.20.cloned.1.call-update) | async-done | bytes 221200
  (536 shorter events, 331.2 us)
Async XLA Ops:
  8.0 395.8 %all-reduce.12.cloned.1.call-start = ((), (), s32[]{:S(2)}) async-start(), calls=%async_computation.6 | async-start | bytes 18874368 | tf_op jit(solution)/shard_map/psum | solution.py:176
  37.3 42.8 %copy-start.92 = (f32[768]{0:T(1024)}, f32[768]{0:T(1024)S(1)}, u32[]{:S(2)}) copy-start(f32[768]{0:T(1024)S(1)} %get-tuple-element.358) | copy-start | bytes 9220
  37.3 42.9 %copy-start.124 = (f32[768]{0:T(1024)}, f32[768]{0:T(1024)S(1)}, u32[]{:S(2)}) copy-start(f32[768]{0:T(1024)S(1)} %get-tuple-element.357) | copy-start | bytes 9220
  40.7 45.2 %copy-start.66 = (f32[3072]{0:T(1024)}, f32[3072]{0:T(1024)S(1)}, u32[]{:S(2)}) copy-start(f32[3072]{0:T(1024)S(1)} %broadcast_multiply_fusion.4) | copy-start | bytes 36868
  43.3 42.7 %copy-start.82 = (f32[3072]{0:T(1024)}, f32[3072]{0:T(1024)S(1)}, u32[]{:S(2)}) copy-start(f32[3072]{0:T(1024)S(1)} %fusion.117) | copy-start | bytes 36868
  91.2 45.9 %copy-start.43 = (f32[3,1024,3]{1,0,2:T(4,128)}, f32[3,1024,3]{1,0,2:T(4,128)S(1)}, u32[]{:S(2)}) copy-start(f32[3,1024,3]{1,0,2:T(4,128)S(1)} %div.265) | copy-start | bytes 110596
  96.3 41.9 %copy-start.26 = (f32[3072,3]{0,1:T(4,128)}, f32[3072,3]{0,1:T(4,128)S(1)}, u32[]{:S(2)}) copy-start(f32[3072,3]{0,1:T(4,128)S(1)} %broadcast_multiply_fusion.1) | copy-start | bytes 110596
  96.3 40.9 %copy-start.11 = (f32[3,1024,3,64]{1,0,3,2:T(4,128)S(1)}, f32[3,1024,3,64]{1,0,3,2:T(4,128)}, u32[]{:S(2)}) copy-start(f32[3,1024,3,64]{1,0,3,2:T(4,128)} %squeeze.65) | copy-start | bytes 7077892
  98.4 41.2 %copy-start.56 = (f32[3072,3]{0,1:T(4,128)}, f32[3072,3]{0,1:T(4,128)S(1)}, u32[]{:S(2)}) copy-start(f32[3072,3]{0,1:T(4,128)S(1)} %multiply_reduce_fusion.10) | copy-start | bytes 110596
  98.5 41.3 %copy-start.45 = (f32[3,1024,3]{1,0,2:T(4,128)}, f32[3,1024,3]{1,0,2:T(4,128)S(1)}, u32[]{:S(2)}) copy-start(f32[3,1024,3]{1,0,2:T(4,128)S(1)} %div.262) | copy-start | bytes 110596
  106.2 36.4 %copy-start.51 = (f32[3,1024,3]{1,0,2:T(4,128)}, f32[3,1024,3]{1,0,2:T(4,128)S(1)}, u32[]{:S(2)}) copy-start(f32[3,1024,3]{1,0,2:T(4,128)S(1)} %add.298) | copy-start | bytes 110596
  106.3 36.4 %copy-start.47 = (f32[3,1024,3]{1,0,2:T(4,128)}, f32[3,1024,3]{1,0,2:T(4,128)S(1)}, u32[]{:S(2)}) copy-start(f32[3,1024,3]{1,0,2:T(4,128)S(1)} %rsqrt.60) | copy-start | bytes 110596
  148.6 48.2 %copy-start.63 = (f32[192,96]{1,0:T(8,128)S(1)}, f32[192,96]{1,0:T(8,128)}, u32[]{:S(2)}) copy-start(f32[192,96]{1,0:T(8,128)} %param.36) | copy-start | bytes 221188
  194.0 40.4 %copy-start.72 = (s32[3,1024]{1,0:T(4,128)}, s32[3,1024]{1,0:T(4,128)S(1)}, u32[]{:S(2)}) copy-start(s32[3,1024]{1,0:T(4,128)S(1)} %get-tuple-element.767) | copy-start | bytes 36868
  196.9 37.5 %copy-start.14 = (bf16[24,8,3,1024]{3,1,2,0:T(8,128)(2,1)}, bf16[24,8,3,1024]{3,1,2,0:T(8,128)(2,1)S(1)}, u32[]{:S(2)}) copy-start(bf16[24,8,3,1024]{3,1,2,0:T(8,128)(2,1)S(1)} %copy.253) | copy-start | bytes 3538948
  234.4 188.9 %all-gather.7.cloned.1.call-start = ((), (), s32[]{:S(2)}) async-start(), calls=%async_computation.7 | async-start | bytes 1327104 | tf_op jit(solution)/shard_map/all_gather | solution.py:142
  236.0 213.6 %all-gather.9.cloned.1.call-start = ((), (), s32[]{:S(2)}) async-start(), calls=%async_computation.8 | async-start | bytes 1327104 | tf_op jit(solution)/shard_map/all_gather | solution.py:143
  236.8 393.1 %all-reduce.14.cloned.1.call-start = ((), (), s32[]{:S(2)}) async-start(), calls=%async_computation.9 | async-start | bytes 18874368 | tf_op jit(solution)/shard_map/psum | solution.py:183
  459.9 384.7 %all-reduce.16.cloned.1.call-start = ((), (), s32[]{:S(2)}) async-start(), calls=%async_computation.10 | async-start | bytes 9437184 | tf_op jit(solution)/shard_map/psum | solution.py:238
  462.0 232.6 %copy-start.111 = (s32[250]{0:T(256)}, s32[250]{0:T(256)S(1)}, u32[]{:S(2)}) copy-start(s32[250]{0:T(256)S(1)} %iota_add_fusion) | copy-start | bytes 3004
  640.8 82.8 %copy-start.57 = (f32[3072]{0:T(1024)}, f32[3072]{0:T(1024)S(1)}, u32[]{:S(2)}) copy-start(f32[3072]{0:T(1024)S(1)} %broadcast_multiply_fusion.2) | copy-start | bytes 36868
  645.8 77.9 %copy-start.68 = (f32[3072]{0:T(1024)}, f32[3072]{0:T(1024)S(1)}, u32[]{:S(2)}) copy-start(f32[3072]{0:T(1024)S(1)} %fusion.119) | copy-start | bytes 36868
  730.8 130.0 %copy-start.102 = (f32[3072]{0:T(1024)}, f32[3072]{0:T(1024)S(1)}, u32[]{:S(2)}) copy-start(f32[3072]{0:T(1024)S(1)} %negate_multiply_fusion.3) | copy-start | bytes 36868
  748.1 96.4 %copy-start.60 = (f32[3072]{0:T(1024)S(1)}, f32[3072]{0:T(1024)}, u32[]{:S(2)}) copy-start(f32[3072]{0:T(1024)} %copy-done.59) | copy-start | bytes 36868
  748.1 96.4 %copy-start.91 = (f32[768]{0:T(1024)S(1)}, f32[768]{0:T(1024)}, u32[]{:S(2)}) copy-start(f32[768]{0:T(1024)} %get-tuple-element.356) | copy-start | bytes 9220
  753.7 485.7 %all-reduce.18.cloned.1.call-start = ((), (), s32[]{:S(2)}) async-start(), calls=%async_computation.11 | async-start | bytes 9437184 | tf_op jit(solution)/shard_map/psum | solution.py:263
  755.1 97.9 %copy-start.87 = (f32[3072]{0:T(1024)S(1)}, f32[3072]{0:T(1024)}, u32[]{:S(2)}) copy-start(f32[3072]{0:T(1024)} %copy-done.86) | copy-start | bytes 36868
  755.1 97.9 %copy-start.76 = (f32[3072]{0:T(1024)S(1)}, f32[3072]{0:T(1024)}, u32[]{:S(2)}) copy-start(f32[3072]{0:T(1024)} %copy-done.75) | copy-start | bytes 36868
  878.4 214.6 %copy-start.27 = (f32[3072,3]{0,1:T(4,128)S(1)}, f32[3072,3]{0,1:T(4,128)}, u32[]{:S(2)}) copy-start(f32[3072,3]{0,1:T(4,128)} %copy-done.26) | copy-start | bytes 110596
  878.4 214.6 %copy-start.101 = (f32[1,3,64]{2,1,0:T(4,128)S(1)}, f32[1,3,64]{2,1,0:T(4,128)}, u32[]{:S(2)}) copy-start(f32[1,3,64]{2,1,0:T(4,128)} %copy-done.99) | copy-start | bytes 2308
  903.8 35.6 %copy-start.2 = (pred[1024,1024]{0,1:T(8,128)(4,1)S(1)}, pred[1024,1024]{0,1:T(8,128)(4,1)}, u32[]{:S(2)}) copy-start(pred[1024,1024]{0,1:T(8,128)(4,1)} %broadcast_compare_fusion.5) | copy-start | bytes 3145732 | tf_op jit(solution)/shard_map/while
  1145.0 130.9 %reduce-scatter.18.cloned.1.call-start = ((), (), s32[]{:S(2)}) async-start(), calls=%async_computation.14 | async-start | bytes 884736 | tf_op jit(solution)/shard_map/reduce_scatter | solution.py:275
  1146.5 158.4 %reduce-scatter.22.cloned.1.call-start = ((), (), s32[]{:S(2)}) async-start(), calls=%async_computation.16 | async-start | bytes 884736
  1153.6 195.0 %reduce-scatter.16.cloned.1.call-start = ((), (), s32[]{:S(2)}) async-start(), calls=%async_computation.13 | async-start | bytes 2654208 | tf_op jit(solution)/shard_map/reduce_scatter | solution.py:274
  1164.5 256.0 %reduce-scatter.14.cloned.1.call-start = ((), (), s32[]{:S(2)}) async-start(), calls=%async_computation.12 | async-start | bytes 2654208 | tf_op jit(solution)/shard_map/reduce_scatter | solution.py:273
  1173.8 65.6 %copy-start.67 = (f32[3072]{0:T(1024)S(1)}, f32[3072]{0:T(1024)}, u32[]{:S(2)}) copy-start(f32[3072]{0:T(1024)} %copy-done.66) | copy-start | bytes 36868
  1173.8 65.6 %copy-start.93 = (f32[768]{0:T(1024)S(1)}, f32[768]{0:T(1024)}, u32[]{:S(2)}) copy-start(f32[768]{0:T(1024)} %copy-done.92) | copy-start | bytes 9220
  1173.8 310.4 %reduce-scatter.24.cloned.1.call-start = ((), (), s32[]{:S(2)}) async-start(), calls=%async_computation.17 | async-start | bytes 442368
  1258.7 294.9 %reduce-scatter.20.cloned.1.call-start = ((), (), s32[]{:S(2)}) async-start(), calls=%async_computation.15 | async-start | bytes 2211840
  1271.5 149.0 %copy-start.36 = (f32[96,768]{1,0:T(8,128)S(1)}, f32[96,768]{1,0:T(8,128)}, u32[]{:S(2)}) copy-start(f32[96,768]{1,0:T(8,128)} %param.39) | copy-start | bytes 884740
  1271.5 149.0 %copy-start.70 = (f32[96,768]{1,0:T(8,128)S(1)}, f32[96,768]{1,0:T(8,128)}, u32[]{:S(2)}) copy-start(f32[96,768]{1,0:T(8,128)} %param.41) | copy-start | bytes 884740
  1271.5 149.0 %copy-start.71 = (f32[96,768]{1,0:T(8,128)S(1)}, f32[96,768]{1,0:T(8,128)}, u32[]{:S(2)}) copy-start(f32[96,768]{1,0:T(8,128)} %param.40) | copy-start | bytes 884740
  1271.5 151.0 %copy-start.83 = (f32[3072]{0:T(1024)S(1)}, f32[3072]{0:T(1024)}, u32[]{:S(2)}) copy-start(f32[3072]{0:T(1024)} %copy-done.82) | copy-start | bytes 36868
  1271.5 151.0 %copy-start.85 = (f32[3072]{0:T(1024)S(1)}, f32[3072]{0:T(1024)}, u32[]{:S(2)}) copy-start(f32[3072]{0:T(1024)} %copy-done.84) | copy-start | bytes 36868
  1422.5 62.6 %copy-start.106 = (f32[7,96]{1,0:T(8,128)S(1)}, f32[7,96]{1,0:T(8,128)}, u32[]{:S(2)}) copy-start(f32[7,96]{1,0:T(8,128)} %param.48) | copy-start | bytes 8068
  1422.5 62.6 %copy-start.119 = (f32[7,96]{1,0:T(8,128)S(1)}, f32[7,96]{1,0:T(8,128)}, u32[]{:S(2)}) copy-start(f32[7,96]{1,0:T(8,128)} %param.50) | copy-start | bytes 8068
  1422.5 62.6 %copy-start.120 = (f32[7,96]{1,0:T(8,128)S(1)}, f32[7,96]{1,0:T(8,128)}, u32[]{:S(2)}) copy-start(f32[7,96]{1,0:T(8,128)} %param.49) | copy-start | bytes 8068
  1485.7 72.1 %copy-start.121 = (f32[7,96]{1,0:T(8,128)}, f32[7,96]{1,0:T(8,128)S(1)}, u32[]{:S(2)}) copy-start(f32[7,96]{1,0:T(8,128)S(1)} %get-tuple-element.422) | copy-start | bytes 8068
  (105 other events, 907.7 us)
Sparse Core Ops, SparseCore 0:
  234.5 169.2 all-reduce.11
  460.0 169.9 all-reduce.13
  753.8 90.7 all-reduce.15
  1145.2 94.2 all-reduce.17
Sparse Core Ops, SparseCore 1:
  237.7 41.0 all-gather.6
  281.3 39.8 all-gather.8
  1148.8 62.7 reduce-scatter.17
  1215.3 61.6 reduce-scatter.21
  1280.4 68.1 reduce-scatter.15
  1352.1 68.3 reduce-scatter.13
  1423.6 60.6 reduce-scatter.23
  1487.6 66.0 reduce-scatter.19
where the time goes:
time: 1580 us; the launch traced here: 1570 us
  waiting for transfers between devices  674 us (43%)
  matrix products  249 us (16%)
  blocking collectives  228 us (14%)
  local copies, waits for them, and re-layouts  203 us (13%)
  other arithmetic  190 us (12%)
  between operations  21.1 us (1%)
    psum x1, waiting for transfers between devices, shards(): attn_sum = lax.psum(head_terms, 'mp')  167 us
    psum x1, waiting for transfers between devices, shards(): mlp_sum = lax.psum(down_terms, 'mp')  136 us
    unnamed x15, waiting for transfers between devices  117 us
    dynamic_update_slice x12, local copies, waits for them, and re-layouts, shards(): lax.map(lambda pieces: attend(pieces[0], pieces[1], pieces[2], pieces[3],...  96.7 us
    psum x1, waiting for transfers between devices, shards(): lax.psum(second_terms.astype(jnp.bfloat16), 'mp').astype(jnp.float32)  89.5 us
    reduce_scatter x1, waiting for transfers between devices, shards(): lax.psum_scatter(grad_up, 'dp', scatter_dimension=0, tiled=True)  69.6 us
    psum x1, waiting for transfers between devices, shards(): lax.psum(first_terms.astype(jnp.bfloat16), 'mp').astype(jnp.float32)  54.1 us
    psum x2, blocking collectives, shards(): loss_sum, image_total = lax.psum((loss_terms, jnp.sum(present)), 'dp')  44.8 us
  transfers between devices with their start and end apart: 12, of which 8 were waited for; matrix products, arithmetic and copies ran while one was open for 10% of the time, Pallas kernels for 0%

commit v1 on v0

v1 whole, which is shorter than its diff:
```python
import functools

import jax
import jax.numpy as jnp
from jax import lax
from jax.experimental import pallas as pl
from jax.experimental.pallas import tpu as pltpu
from jax.sharding import PartitionSpec as P

LEN = 1024
STEP = 10
SEQ_DEV = 3
IMG_DEV = 180
PAD_ID = 180

NORM_EPS = 1e-06
MASK_FILL = -1000000000.0
BETA_ONE = 0.9
BETA_TWO = 0.999
ADAM_EPS = 1e-08
MATRIX_RATE = 0.1
MATRIX_DECAY = 0.1
GAIN_RATE = 0.8

HEAD = 64
QB = 128
QBLOCKS = LEN // QB
WINDOWS = (384, 640, 1024)
F32 = jnp.float32
BF16 = jnp.bfloat16
VMEM_LIMIT = 56 * 1024 * 1024
IMG_SEQ = 60
SLOTS = 64
ANY = pl.BlockSpec(memory_space=pl.ANY)
PARAMS = pltpu.CompilerParams(vmem_limit_bytes=VMEM_LIMIT)


def dot(a, b, ca, cb):
    return lax.dot_general(a, b, (((ca,), (cb,)), ((), ())), preferred_element_type=F32)


def head_mean(values, ones_block):
    high = values.astype(BF16)
    rest = (values - high.astype(F32)).astype(BF16)
    return dot(high, ones_block, 1, 0) + dot(rest, ones_block, 1, 0)


def norm_parts(values):
    centre = values - jnp.mean(values, axis=-1, keepdims=True)
    spread = jnp.mean(centre * centre, axis=-1, keepdims=True)
    scale = lax.rsqrt(spread + NORM_EPS)
    return centre * scale, scale


def norm_back(grad, normed, scale, gain):
    scaled = grad * gain
    first = jnp.mean(scaled, axis=-1, keepdims=True)
    second = jnp.mean(scaled * normed, axis=-1, keepdims=True)
    return (scaled - first - normed * second) * scale


def head_parts(values, ones_block):
    centre = values - head_mean(values, ones_block)
    scale = lax.rsqrt(head_mean(centre * centre, ones_block) + NORM_EPS)
    return centre * scale, scale


def cost(flops, read, exps=0):
    return pl.CostEstimate(flops=int(flops), bytes_accessed=int(read), transcendentals=int(exps))


def whole(shape):
    return pl.BlockSpec(tuple(shape), lambda *_: (0,) * len(shape))


class Plan:
    def __init__(self, n_dp, n_mp, dim):
        self.n_dp, self.n_mp = n_dp, n_mp
        self.merge = 1 if dim // n_dp % 16 == 0 else 2
        self.groups = n_dp // self.merge
        self.block = dim // self.groups
        self.far = [2 * k for k in range(1, self.groups // 2)]

    def swap(self, value, axis, bits):
        size = self.n_dp if axis == "dp" else self.n_mp
        return lax.ppermute(value, axis, [(i, i ^ bits) for i in range(size)])

    def group_swap(self, value, bits):
        return self.swap(value, "dp", bits * self.merge)

    def merged(self, value, dim):
        if self.merge == 1:
            return value
        other = self.swap(value, "dp", 1)
        even = lax.axis_index("dp") % 2 == 0
        first, second = jnp.where(even, value, other), jnp.where(even, other, value)
        return jnp.concatenate([first, second], axis=dim)

    def unmerged(self, value, dim):
        if self.merge == 1:
            return value
        half = value.shape[dim] // 2
        me = lax.axis_index("dp") % 2
        mine = lax.dynamic_slice_in_dim(value, me * half, half, dim)
        theirs = lax.dynamic_slice_in_dim(value, (1 - me) * half, half, dim)
        return mine + self.swap(theirs, "dp", 1)

    def gather(self, block, order, after=None):
        value, places = block[None], [(0, 0)]
        for step in order:
            if step == "x":
                got = [(self.swap(value, "mp", 2), 0, 2)]
            elif step == "y":
                got = [(self.group_swap(value, 1), 1, 0)]
            else:
                got = [(self.group_swap(value, k), k, 0) for k in self.far]
            value = jnp.concatenate([value] + [g for g, _, _ in got], axis=0)
            places = places + [(a ^ i, b ^ j) for _, i, j in got for a, b in places]
        return value, places

    def both_cores(self, gathered):
        value, places = gathered
        return [gathered, (self.swap(value, "mp", 1), [(a, b ^ 1) for a, b in places])]

    def scatter(self, keep, send, order):
        value = keep.astype(F32) + self.swap(send, "mp", 1).astype(F32)
        return self.scatter_rest(value, "xyz", order, 0)

    def scatter_rest(self, value, axes, order, row_dim):
        for step in order:
            at = axes.index(step)
            axes = axes[:at] + axes[at + 1 :]
            low = value.astype(BF16)
            count = value.shape[at]
            parts = [lax.index_in_dim(low, k, at, keepdims=False) for k in range(1, count)]
            value = lax.index_in_dim(value, 0, at, keepdims=False)
            for k, part in enumerate(parts, start=1):
                if step == "x":
                    got = self.swap(part, "mp", 2)
                else:
                    got = self.group_swap(part, k if step == "y" else 2 * k)
                value = value + got.astype(F32)
        return self.unmerged(value, row_dim)

    def total(self, value, axis):
        size = self.n_dp if axis == "dp" else self.n_mp
        bits = 1
        while bits < size:
            value = value + self.swap(value, axis, bits)
            bits *= 2
        return value


def copy_blocks(pieces, target, sems, first):
    copies = []
    for ref, places in pieces:
        for i, (group, other) in enumerate(places):
            source, dest = target(ref, i, group, other)
            copies.append(pltpu.make_async_copy(source, dest, sems.at[first + len(copies)]))
    return copies


def start_all(copies):
    for c in copies:
        c.start()


def wait_all(copies):
    for c in copies:
        c.wait()


def project(plan, ids, tokens, qk_pieces, v_pieces, params, gains, ones):
    rows, dim = tokens.shape
    cols = ones.shape[0]
    block = 512
    size = plan.block

    def kernel(ids_ref, x_ref, norm_ref, gain_ref, ones_ref, qk_ref, v_in_ref, low_ref, pq_ref, pk_ref, q_ref, k_ref, v_ref, w_ref, sems):
        me = ids_ref[0]

        def place(slot, count):
            def target(ref, i, group, other):
                rows_at = pl.ds(pl.multiple_of((me ^ group) * size, 16), size)
                return ref.at[i], w_ref.at[pl.ds(slot, count), rows_at, :]

            return target

        copies = copy_blocks([(qk_ref, qk_pieces[1])], place(0, 2), sems, 0)
        copies += copy_blocks([(v_in_ref, v_pieces[1])], place(2, 1), sems, len(copies))
        pl.when(pl.program_id(0) == 0)(lambda: start_all(copies))
        normed, _ = norm_parts(x_ref[...].astype(F32))
        low = (normed * norm_ref[0:1, :] + norm_ref[1:2, :]).astype(BF16)
        low_ref[...] = low
        pl.when(pl.program_id(0) == 0)(lambda: wait_all(copies))
        ones_block = ones_ref[...]
        pq = dot(low, w_ref[0], 1, 0)
        pk = dot(low, w_ref[1], 1, 0)
        pq_ref[...] = pq
        pk_ref[...] = pk
        v_ref[...] = dot(low, w_ref[2], 1, 0).astype(BF16)
        nq, _ = head_parts(pq, ones_block)
        nk, _ = head_parts(pk, ones_block)
        q_ref[...] = (nq * gain_ref[0:1, :]).astype(BF16)
        k_ref[...] = (nk * gain_ref[1:2, :]).astype(BF16)

    row = lambda c: pl.BlockSpec((block, c), lambda i, *_: (i, 0))
    shape = lambda c, t: jax.ShapeDtypeStruct((rows, c), t)
    return pl.pallas_call(
        kernel,
        grid_spec=pltpu.PrefetchScalarGridSpec(
            num_scalar_prefetch=1,
            grid=(rows // block,),
            in_specs=[row(dim), whole(params.shape), whole(gains.shape), whole(ones.shape), ANY, ANY],
            out_specs=[row(dim), row(cols), row(cols), row(cols), row(cols), row(cols)],
            scratch_shapes=[pltpu.VMEM((3, dim, cols), BF16), pltpu.SemaphoreType.DMA((2 * plan.groups,))],
        ),
        out_shape=[shape(dim, BF16), shape(cols, F32), shape(cols, F32), shape(cols, BF16), shape(cols, BF16), shape(cols, BF16)],
        compiler_params=PARAMS,
        cost_estimate=cost(6 * rows * dim * cols, rows * dim * 8),
        name="project",
    )(ids, tokens, params, gains, ones, qk_pieces[0], v_pieces[0])


def head_masks(cols):
    lane = lax.broadcasted_iota(jnp.int32, (1, cols), 1)
    return [(lane >= h * HEAD) & (lane < (h + 1) * HEAD) for h in range(cols // HEAD)]


def spread_heads(block, masks):
    zero = jnp.zeros_like(block)
    return jnp.concatenate([jnp.where(m, block, zero) for m in masks], axis=0)


def join_heads(stacked, masks):
    total = stacked[0:QB]
    for h in range(1, len(masks)):
        total = jnp.where(masks[h], stacked[h * QB : (h + 1) * QB], total)
    return total


def by_window(width_ref, step, body):
    width = width_ref[step]
    for number, window in enumerate(WINDOWS):
        pl.when(width == number)(functools.partial(body, window))


def seq_specs(seq, cols):
    block = lambda c: pl.BlockSpec((QB, c), lambda b, *_: (seq * QBLOCKS + b, 0))
    all_keys = lambda c: pl.BlockSpec((LEN, c), lambda b, *_: (seq, 0))
    seg_row = pl.BlockSpec((1, 1, LEN), lambda b, *_: (seq, 0, 0))
    return block, all_keys, seg_row


def attend(plan, seq, ids, starts, widths, q, k, v, seg_col, seg_row):
    rows, cols = q.shape
    n_mp = plan.n_mp
    share = LEN // n_mp
    per = share // QB

    def kernel(ids_ref, start_ref, width_ref, q_ref, k_ref, v_ref, col_ref, row_ref, *outs):
        out_refs, log_ref = outs[:n_mp], outs[n_mp]
        block = pl.program_id(0)
        step = seq * QBLOCKS + block
        masks = head_masks(cols)
        heads = len(masks)

        def body(window):
            start = pl.multiple_of(start_ref[step], QB)
            keys = k_ref[pl.ds(start, window), :]
            values = v_ref[pl.ds(start, window), :]
            q3 = spread_heads(q_ref[...], masks)
            s = (dot(q3, keys, 1, 1) * HEAD**-0.5).reshape(heads, QB, window)
            same = col_ref[...] == row_ref[0, :, pl.ds(start, window)]
            s = jnp.where(same[None], s, MASK_FILL)
            top = jnp.max(s, axis=-1, keepdims=True)
            e = jnp.exp(s - top)
            total = jnp.sum(e, axis=-1, keepdims=True)
            p = (e * (1.0 / total)).astype(BF16).reshape(heads * QB, window)
            out = join_heads(dot(p, values, 1, 0), masks).astype(BF16)
            other = (block // per) ^ ids_ref[1]
            at = pl.ds(pl.multiple_of(block % per * QB, QB), QB)
            for r in range(n_mp):

                @pl.when(other == r)
                def _():
                    out_refs[r][at, :] = out

            log = top + jnp.log(total)
            lane = lax.broadcasted_iota(jnp.int32, (QB, 128), 1)
            logs = jnp.zeros((QB, 128), F32)
            for h in range(heads):
                logs = jnp.where(lane == h, log[h], logs)
            log_ref[...] = logs

        by_window(width_ref, step, body)

    block, all_keys, row_spec = seq_specs(seq, cols)
    return pl.pallas_call(
        kernel,
        grid_spec=pltpu.PrefetchScalarGridSpec(
            num_scalar_prefetch=3,
            grid=(QBLOCKS,),
            in_specs=[block(cols), all_keys(cols), all_keys(cols), block(1), row_spec],
            out_specs=[whole((share, cols))] * n_mp + [pl.BlockSpec((QB, 128), lambda b, *_: (b, 0))],
        ),
        out_shape=[jax.ShapeDtypeStruct((share, cols), BF16)] * n_mp + [jax.ShapeDtypeStruct((LEN, 128), F32)],
        compiler_params=PARAMS,
        cost_estimate=cost(4 * LEN * LEN * cols, LEN * cols * 8, LEN * LEN),
        name="attend",
    )(ids, starts, widths, q, k, v, seg_col, seg_row)


def attend_back(plan, seq, ids, starts, widths, live, q, k, v, grads, logs, seg_col, seg_row):
    rows, cols = q.shape
    n_mp = plan.n_mp
    share = LEN // n_mp
    per = share // QB

    def kernel(ids_ref, start_ref, width_ref, live_ref, q_ref, k_ref, v_ref, col_ref, row_ref, log_ref, *refs):
        grad_refs, (dq_ref, dk_ref, dv_ref) = refs[:n_mp], refs[n_mp:]
        block = pl.program_id(0)
        step = seq * QBLOCKS + block
        masks = head_masks(cols)
        heads = len(masks)

        @pl.when(block == 0)
        def _():
            dk_ref[...] = jnp.zeros_like(dk_ref)
            dv_ref[...] = jnp.zeros_like(dv_ref)

        def body(window):
            start = pl.multiple_of(start_ref[step], QB)
            keys = pl.ds(start, window)
            k_win = k_ref[keys, :]
            v_win = v_ref[keys, :]
            other = (block // per) ^ ids_ref[1]
            at = pl.ds(pl.multiple_of(block % per * QB, QB), QB)
            g = grad_refs[0][at, :]
            for r in range(1, n_mp):
                g = jnp.where(other == r, grad_refs[r][at, :], g)
            q3 = spread_heads(q_ref[...], masks)
            g3 = spread_heads(g, masks)
            s = (dot(q3, k_win, 1, 1) * HEAD**-0.5).reshape(heads, QB, window)
            same = col_ref[...] == row_ref[0, :, keys]
            all_logs = log_ref[...]
            log = jnp.stack([all_logs[:, h : h + 1] for h in range(heads)])
            p = jnp.exp(jnp.where(same[None], s - log, MASK_FILL))
            dp = dot(g3, v_win, 1, 1).reshape(heads, QB, window)
            inner = jnp.sum(p * dp, axis=-1, keepdims=True)
            ds = (p * (dp - inner)).astype(BF16).reshape(heads * QB, window)
            p_low = p.astype(BF16).reshape(heads * QB, window)
            dv_ref[keys, :] += dot(p_low, g3, 0, 0)
            dk_ref[keys, :] += dot(ds, q3, 0, 0) * HEAD**-0.5
            dq_ref[...] = join_heads(dot(ds, k_win, 1, 0), masks) * HEAD**-0.5

        alive = live_ref[step]

        @pl.when(alive == 0)
        def _():
            dq_ref[...] = jnp.zeros_like(dq_ref)

        @pl.when(alive != 0)
        def _():
            by_window(width_ref, step, body)

    block, all_keys, row_spec = seq_specs(seq, cols)
    grad_spec = pl.BlockSpec((share, cols), lambda b, *_: (seq, 0))
    shape = jax.ShapeDtypeStruct((LEN, cols), F32)
    return pl.pallas_call(
        kernel,
        grid_spec=pltpu.PrefetchScalarGridSpec(
            num_scalar_prefetch=4,
            grid=(QBLOCKS,),
            in_specs=[block(cols), all_keys(cols), all_keys(cols), block(1), row_spec, pl.BlockSpec((QB, 128), lambda b, *_: (b, 0))]
            + [grad_spec] * n_mp,
            out_specs=[pl.BlockSpec((QB, cols), lambda b, *_: (b, 0)), whole((LEN, cols)), whole((LEN, cols))],
        ),
        out_shape=[shape, shape, shape],
        compiler_params=PARAMS,
        cost_estimate=cost(10 * LEN * LEN * cols, LEN * cols * 24, LEN * LEN),
        name="attend_back",
    )(ids, starts, widths, live, q, k, v, seg_col, seg_row, logs, *grads)


def key_windows(seg_ids):
    seg = seg_ids.reshape(-1, LEN)
    first = seg[:, ::QB]
    last = seg[:, QB - 1 :: QB]
    low = jnp.sum((seg[:, None, :] < first[:, :, None]).astype(jnp.int32), axis=2)
    high = jnp.sum((seg[:, None, :] <= last[:, :, None]).astype(jnp.int32), axis=2)
    base = low // QB * QB
    number = jnp.full(base.shape, len(WINDOWS) - 1, jnp.int32)
    start = jnp.zeros_like(base)
    for choice in range(len(WINDOWS) - 2, -1, -1):
        at = jnp.minimum(base, LEN - WINDOWS[choice])
        fits = high <= at + WINDOWS[choice]
        number = jnp.where(fits, choice, number)
        start = jnp.where(fits, at, start)
    live = (first != PAD_ID).astype(jnp.int32)
    return start.reshape(-1), number.reshape(-1), live.reshape(-1)


def project_back(plan, seq, ids, low, pq, pk, dq, dk, dv, w_grad, qk_pieces, v_pieces, gains, ones):
    rows, dim = low.shape
    cols = ones.shape[0]
    n_mp = plan.n_mp
    share = LEN // n_mp
    size = plan.block
    half = n_mp // 2

    def kernel(ids_ref, low_ref, pq_ref, pk_ref, dq_ref, dk_ref, dv_ref, gain_ref, ones_ref, qk_ref, v_in_ref, *rest):
        if w_grad is not None:
            base_ref, base_gain_ref = rest[:2]
            rest = rest[2:]
        keep_ref, send_ref, grad_ref, gains_ref, w_ref, sems = rest
        me = ids_ref[0]
        step = pl.program_id(0)

        def place(slot, count):
            def target(ref, i, group, other):
                rows_at = pl.ds(pl.multiple_of((me ^ group) * size, 16), size)
                return ref.at[i], w_ref.at[pl.ds(slot, count), rows_at, :]

            return target

        copies = copy_blocks([(qk_ref, qk_pieces[1])], place(0, 2), sems, 0)
        copies += copy_blocks([(v_in_ref, v_pieces[1])], place(2, 1), sems, len(copies))

        @pl.when(step == 0)
        def _():
            start_all(copies)
            if w_grad is None:
                grad_ref[...] = jnp.zeros_like(grad_ref)
                gains_ref[...] = jnp.zeros_like(gains_ref)
            else:
                grad_ref[...] = base_ref[...]
                gains_ref[...] = base_gain_ref[...]

        ones_block = ones_ref[...]

        def back(values, grad, gain, slot):
            normed, scale = head_parts(values, ones_block)
            gains_ref[slot, :, :] += jnp.sum((grad * normed).reshape(-1, 8, cols), axis=0)
            scaled = grad * gain
            first = head_mean(scaled, ones_block)
            second = head_mean(scaled * normed, ones_block)
            return ((scaled - first - normed * second) * scale).astype(BF16)

        gq = back(pq_ref[...], dq_ref[...], gain_ref[0:1, :], 0)
        gk = back(pk_ref[...], dk_ref[...], gain_ref[1:2, :], 1)
        gv = dv_ref[...].astype(BF16)
        x = low_ref[...]
        pl.when(step == 0)(lambda: wait_all(copies))
        terms = dot(gq, w_ref[0], 1, 1) + dot(gk, w_ref[1], 1, 1) + dot(gv, w_ref[2], 1, 1)
        terms = terms.astype(BF16)

        @pl.when(step < half)
        def _():
            keep_ref[...] = terms

        @pl.when(step >= half)
        def _():
            send_ref[...] = terms

        for p, g in enumerate((gq, gk, gv)):
            grad_ref[p] += dot(x, g, 0, 0)

    at = lambda i, ids_ref: ids_ref[1] ^ (i % half * 2 + i // half)
    far = lambda c: pl.BlockSpec((share, c), lambda i, ids_ref: (seq * n_mp + at(i, ids_ref), 0))
    near = lambda c: pl.BlockSpec((share, c), lambda i, ids_ref: (at(i, ids_ref), 0))
    w_shape, g_shape = (3, dim, cols), (2, 8, cols)
    base = [] if w_grad is None else list(w_grad)
    return pl.pallas_call(
        kernel,
        grid_spec=pltpu.PrefetchScalarGridSpec(
            num_scalar_prefetch=1,
            grid=(n_mp,),
            in_specs=[far(dim), far(cols), far(cols), near(cols), near(cols), near(cols), whole(gains.shape), whole(ones.shape), ANY, ANY]
            + [whole(b.shape) for b in base],
            out_specs=[
                pl.BlockSpec((None, share, dim), lambda i, *_: (jnp.minimum(i, half - 1), 0, 0)),
                pl.BlockSpec((None, share, dim), lambda i, *_: (jnp.maximum(i - half, 0), 0, 0)),
                whole(w_shape),
                whole(g_shape),
            ],
            scratch_shapes=[pltpu.VMEM(w_shape, BF16), pltpu.SemaphoreType.DMA((2 * plan.groups,))],
        ),
        out_shape=[
            jax.ShapeDtypeStruct((half, share, dim), BF16),
            jax.ShapeDtypeStruct((half, share, dim), BF16),
            jax.ShapeDtypeStruct(w_shape, F32),
            jax.ShapeDtypeStruct(g_shape, F32),
        ],
        compiler_params=PARAMS,
        cost_estimate=cost(12 * LEN * dim * cols, LEN * dim * 12),
        name="project_back",
    )(ids, low, pq, pk, dq, dk, dv, gains, ones, qk_pieces[0], v_pieces[0], *base)


def out_target(plan, me, out_ref):
    def target(ref, i, group, other):
        rows_at = pl.ds(pl.multiple_of((me ^ group) * plan.block, 16), plan.block)
        return ref.at[i, :, pl.ds(0, out_ref.shape[2])], out_ref.at[other, rows_at, :]

    return target


def wide_target(plan, me, mp, w_ref, source_col=None):
    width = w_ref.shape[1] // plan.n_mp

    def target(ref, i, group, other):
        rows_at = pl.ds(pl.multiple_of((me ^ group) * plan.block, 16), plan.block)
        cols_at = pl.ds(pl.multiple_of((mp ^ other) * width, 128), width)
        source = ref.at[i] if source_col is None else ref.at[i, :, pl.ds(source_col, width)]
        return source, w_ref.at[rows_at, cols_at]

    return target


def blocks_of(pieces):
    return sum(len(places) for _, places in pieces)


def feed_up(plan, ids, x, attended, params, oc, up, out_cols):
    rows, dim = x.shape
    cols = attended[0].shape[1]
    n_mp = plan.n_mp
    width = up[0][0].shape[2]
    hidden_size = n_mp * width
    block = 256

    def kernel(ids_ref, x_ref, *refs):
        a_refs, refs = refs[:n_mp], refs[n_mp:]
        norm_ref, oc_a, oc_b, up_a, up_b, mid_ref, low_ref, act_ref, der_ref, o_ref, u_ref, sems = refs
        me, mp = ids_ref[0], ids_ref[1]
        first = pl.program_id(0) == 0
        o_copies = copy_blocks([(oc_a, oc[0][1]), (oc_b, oc[1][1])], out_target(plan, me, o_ref), sems, 0)
        u_copies = copy_blocks([(up_a, up[0][1]), (up_b, up[1][1])], wide_target(plan, me, mp, u_ref), sems, len(o_copies))

        @pl.when(first)
        def _():
            start_all(o_copies)
            start_all(u_copies)
            wait_all(o_copies)

        middle = x_ref[...].astype(F32)
        for r in range(n_mp):
            middle = middle + dot(a_refs[r][...], o_ref[r, :, :cols], 1, 1)
        mid_ref[...] = middle
        normed, _ = norm_parts(middle)
        low = (normed * norm_ref[2:3, :] + norm_ref[3:4, :]).astype(BF16)
        low_ref[...] = low
        pl.when(first)(lambda: wait_all(u_copies))
        for c in range(n_mp):
            at = slice(c * width, (c + 1) * width)
            hidden = dot(low, u_ref[:, at], 1, 0)
            phi = 0.5 * (1.0 + lax.erf(hidden * (0.5**0.5)))
            act_ref[:, at] = (hidden * phi).astype(BF16)
            der_ref[:, at] = phi + hidden * (jnp.exp(-0.5 * hidden * hidden) * 0.3989422804014327)

    row = lambda c: pl.BlockSpec((block, c), lambda i, *_: (i, 0))
    shape = lambda c, t: jax.ShapeDtypeStruct((rows, c), t)
    return pl.pallas_call(
        kernel,
        grid_spec=pltpu.PrefetchScalarGridSpec(
            num_scalar_prefetch=1,
            grid=(rows // block,),
            in_specs=[row(dim)] + [row(cols)] * n_mp + [whole(params.shape)] + [ANY] * 4,
            out_specs=[row(dim), row(dim), row(hidden_size), row(hidden_size)],
            scratch_shapes=[
                pltpu.VMEM((n_mp, dim, out_cols), BF16),
                pltpu.VMEM((dim, hidden_size), BF16),
                pltpu.SemaphoreType.DMA((blocks_of(oc) + blocks_of(up),)),
            ],
        ),
        out_shape=[shape(dim, F32), shape(dim, BF16), shape(hidden_size, BF16), shape(hidden_size, F32)],
        compiler_params=PARAMS,
        cost_estimate=cost(2 * rows * dim * (hidden_size + dim), rows * hidden_size * 8, rows * hidden_size * 2),
        name="feed_up",
    )(ids, x, *attended, params, oc[0][0], oc[1][0], up[0][0], up[1][0])


def image_rows(seq_block, shape, axis):
    slot = lax.broadcasted_iota(jnp.int32, shape, axis)
    return slot, seq_block * IMG_SEQ


def feed_down(plan, ids, middle, active, seg_row, params, down):
    rows, dim = middle.shape
    n_mp = plan.n_mp
    hidden_size = active.shape[1]
    block = 256
    seqs = rows // block

    def kernel(ids_ref, mid_ref, act_ref, seg_ref, norm_ref, d_a, d_b, res_ref, block_ref, pool_ref, d_ref, sems):
        me, mp = ids_ref[0], ids_ref[1]
        seq = pl.program_id(0)
        copies = copy_blocks([(d_a, down[0][1]), (d_b, down[1][1])], wide_target(plan, me, mp, d_ref), sems, 0)

        @pl.when(seq == 0)
        def _():
            start_all(copies)
            wait_all(copies)

        result = mid_ref[...] + dot(act_ref[...], d_ref[...], 1, 1)
        res_ref[...] = result
        block_ref[...] = result.astype(BF16)
        normed, _ = norm_parts(result)
        final = normed * norm_ref[4:5, :] + norm_ref[5:6, :]
        probe = jnp.broadcast_to(norm_ref[6:7, :], (8, dim))
        score = lax.dot_general(
            probe, final, (((1,), (1,)), ((), ())), precision=lax.Precision.HIGHEST, preferred_element_type=F32
        )[0:1]
        slot = lax.broadcasted_iota(jnp.int32, (SLOTS, block), 0)
        member = (seg_ref[0] - seq * IMG_SEQ == slot) & (slot < IMG_SEQ)
        top = jnp.max(jnp.where(member, score, MASK_FILL), axis=1, keepdims=True)
        e = jnp.exp(jnp.where(member, score - top, MASK_FILL))
        e = jnp.where(member, e, 0.0)
        total = jnp.sum(e, axis=1, keepdims=True)
        low = final.astype(BF16)
        high = e.astype(BF16)
        rest = (e - high.astype(F32)).astype(BF16)
        pool_ref[:, :dim] = dot(high, low, 1, 0) + dot(rest, low, 1, 0)
        lane = lax.broadcasted_iota(jnp.int32, (SLOTS, 128), 1)
        pool_ref[:, dim:] = jnp.where(lane == 0, top, jnp.where(lane == 1, total, 0.0))

    row = lambda c: pl.BlockSpec((block, c), lambda i, *_: (i, 0))
    return pl.pallas_call(
        kernel,
        grid_spec=pltpu.PrefetchScalarGridSpec(
            num_scalar_prefetch=1,
            grid=(seqs,),
            in_specs=[row(dim), row(hidden_size), pl.BlockSpec((1, 1, block), lambda i, *_: (i, 0, 0)), whole(params.shape), ANY, ANY],
            out_specs=[row(dim), row(dim), pl.BlockSpec((SLOTS, dim + 128), lambda i, *_: (i, 0))],
            scratch_shapes=[pltpu.VMEM((dim, hidden_size), BF16), pltpu.SemaphoreType.DMA((blocks_of(down),))],
        ),
        out_shape=[
            jax.ShapeDtypeStruct((rows, dim), F32),
            jax.ShapeDtypeStruct((rows, dim), BF16),
            jax.ShapeDtypeStruct((seqs * SLOTS, dim + 128), F32),
        ],
        compiler_params=PARAMS,
        cost_estimate=cost(2 * rows * dim * hidden_size, rows * hidden_size * 4),
        name="feed_down",
    )(ids, middle, active, seg_row, params, down[0][0], down[1][0])


def combine_pools(plan, pool, bits, dim):
    other = plan.swap(pool, "mp", bits)
    lower = lax.axis_index("mp") & bits == 0
    first, second = jnp.where(lower, pool, other), jnp.where(lower, other, pool)
    top_a, top_b = first[:, dim : dim + 1], second[:, dim : dim + 1]
    top = jnp.maximum(top_a, top_b)
    weight_a, weight_b = jnp.exp(top_a - top), jnp.exp(top_b - top)
    rows = first[:, :dim] * weight_a + second[:, :dim] * weight_b
    total = first[:, dim + 1 : dim + 2] * weight_a + second[:, dim + 1 : dim + 2] * weight_b
    pad = jnp.zeros((pool.shape[0], pool.shape[1] - dim - 2), F32)
    return jnp.concatenate([rows, top, total, pad], axis=1)


def classify(plan, ids, pool, labels, images, oc, class_count, class_cols, source_col):
    slots, full = pool.shape
    dim = full - 128
    n_mp = plan.n_mp
    wide = n_mp * class_cols

    def kernel(ids_ref, pool_ref, label_ref, images_ref, c_a, c_b, grad_ref, stat_ref, loss_ref, cls_ref, c_ref, l_ref, sems):
        me, mp = ids_ref[0], ids_ref[1]
        copies = copy_blocks([(c_a, oc[0][1]), (c_b, oc[1][1])], wide_target(plan, me, mp, c_ref, source_col), sems, 0)
        start_all(copies)
        top = pool_ref[:, dim : dim + 1]
        total = pool_ref[:, dim + 1 : dim + 2]
        present = jnp.where(total > 0, 1.0, 0.0)
        safe = total + (1.0 - present)
        pooled = pool_ref[:, :dim] / safe
        low = pooled.astype(BF16)
        wait_all(copies)
        logits = dot(low, c_ref[...], 1, 0)
        column = lax.broadcasted_iota(jnp.int32, (slots, wide), 1)
        logits = jnp.where(column % class_cols < class_count, logits, MASK_FILL)
        row_top = jnp.max(logits, axis=1, keepdims=True)
        log_total = row_top + jnp.log(jnp.sum(jnp.exp(logits - row_top), axis=1, keepdims=True))
        chosen = jnp.where(column == label_ref[...], 1.0, 0.0)
        label_logit = jnp.sum(chosen * logits, axis=1, keepdims=True)
        loss = jnp.sum(present * (log_total - label_logit), axis=0, keepdims=True)
        loss_ref[...] = jnp.broadcast_to(loss, loss_ref.shape)
        scale = present / images_ref[0:1, 0:1]
        grad = ((jnp.exp(logits - log_total) - chosen) * scale).astype(BF16)
        l_ref[...] = grad
        row_grad = dot(grad, c_ref[...], 1, 1).astype(BF16)
        grad_ref[...] = row_grad
        inner = jnp.sum(row_grad.astype(F32) * pooled, axis=1, keepdims=True)
        lane = lax.broadcasted_iota(jnp.int32, (slots, 128), 1)
        stat_ref[...] = jnp.where(lane == 0, top, jnp.where(lane == 1, 1.0 / safe, jnp.where(lane == 2, inner, 0.0)))
        own = l_ref[:, pl.ds(pl.multiple_of(mp * class_cols, 128), class_cols)]
        grad_cls = dot(low, own, 0, 0)
        for g in range(plan.groups):
            r = g ^ me
            at = (r & 1) * (plan.groups // 2) + (r >> 1)
            cls_ref[at] = grad_cls[g * plan.block : (g + 1) * plan.block].astype(BF16)

    vmem = pl.BlockSpec(memory_space=pltpu.VMEM)
    return pl.pallas_call(
        kernel,
        in_specs=[pl.BlockSpec(memory_space=pltpu.SMEM), vmem, vmem, vmem, ANY, ANY],
        out_specs=[vmem] * 4,
        out_shape=[
            jax.ShapeDtypeStruct((slots, dim), BF16),
            jax.ShapeDtypeStruct((slots, 128), F32),
            jax.ShapeDtypeStruct((8, 128), F32),
            jax.ShapeDtypeStruct((plan.groups, plan.block, class_cols), BF16),
        ],
        scratch_shapes=[
            pltpu.VMEM((dim, wide), BF16),
            pltpu.VMEM((slots, wide), BF16),
            pltpu.SemaphoreType.DMA((blocks_of(oc),)),
        ],
        compiler_params=PARAMS,
        cost_estimate=cost(6 * slots * dim * wide, dim * wide * 2),
        name="classify",
    )(ids, pool, labels, images, oc[0][0], oc[1][0])


def split_three(values):
    high = values.astype(BF16)
    rest = values - high.astype(F32)
    middle = rest.astype(BF16)
    low = (rest - middle.astype(F32)).astype(BF16)
    return high, middle, low


def feed_back(plan, ids, result, middle, slope, row_grads, stats, seg_col, params, oc, up, down, out_cols, cols):
    rows, dim = result.shape
    n_mp = plan.n_mp
    width = up[0][0].shape[2]
    hidden_size = n_mp * width
    block = 256

    def kernel(ids_ref, res_ref, mid_ref, der_ref, pg_ref, stat_ref, seg_ref, norm_ref, oc_a, oc_b, u_a, u_b, d_a, d_b, *refs):
        rlow_ref, hlow_ref, mlow_ref, mgrad_ref, *refs = refs
        ag_refs, (sums_ref, o_ref, u_ref, d_ref, sems) = refs[:n_mp], refs[n_mp:]
        me, mp = ids_ref[0], ids_ref[1]
        seq = pl.program_id(0)
        d_copies = copy_blocks([(d_a, down[0][1]), (d_b, down[1][1])], wide_target(plan, me, mp, d_ref), sems, 0)
        u_copies = copy_blocks([(u_a, up[0][1]), (u_b, up[1][1])], wide_target(plan, me, mp, u_ref), sems, len(d_copies))
        o_copies = copy_blocks(
            [(oc_a, oc[0][1]), (oc_b, oc[1][1])], out_target(plan, me, o_ref), sems, len(d_copies) + len(u_copies)
        )

        @pl.when(seq == 0)
        def _():
            start_all(d_copies)
            start_all(u_copies)
            start_all(o_copies)
            sums_ref[...] = jnp.zeros_like(sums_ref)

        normed, scale = norm_parts(res_ref[...])
        gain, probe = norm_ref[4:5, :], norm_ref[6:7, :]
        final = normed * gain + norm_ref[5:6, :]
        score = jnp.sum(final * probe, axis=1, keepdims=True)
        slot = lax.broadcasted_iota(jnp.int32, (block, SLOTS), 1)
        member = (seg_ref[...] - seq * IMG_SEQ == slot) & (slot < IMG_SEQ)
        held = jnp.max(jnp.where(member, 1.0, 0.0), axis=1, keepdims=True)
        one = jnp.where(member, 1.0, 0.0).astype(BF16)
        row_stat = sum(dot(one, part, 1, 0) for part in split_three(stat_ref[...]))
        top, inverse, inner = row_stat[:, 0:1], row_stat[:, 1:2], row_stat[:, 2:3]
        share = jnp.exp(jnp.where(held > 0, score - top, 0.0)) * inverse * held
        row_grad = dot(one, pg_ref[...], 1, 0)
        share_low = share.astype(BF16).astype(F32)
        share_grad = jnp.sum(row_grad * final.astype(BF16).astype(F32), axis=1, keepdims=True)
        score_grad = share * (share_grad - inner)
        final_grad = share_low * row_grad + score_grad * probe
        add = lambda slot, value: sums_ref.at[slot].__setitem__(
            ..., sums_ref[slot] + jnp.sum(value.reshape(-1, 8, dim), axis=0)
        )
        add(4, score_grad * final)
        add(2, final_grad * normed)
        add(3, final_grad)
        result_grad = norm_back(final_grad, normed, scale, gain)
        result_low = result_grad.astype(BF16)
        rlow_ref[...] = result_low
        pl.when(seq == 0)(lambda: (wait_all(d_copies), wait_all(u_copies), wait_all(o_copies)) and None)
        second = jnp.zeros((block, dim), F32)
        for c in range(n_mp):
            at = slice(c * width, (c + 1) * width)
            hidden_low = (der_ref[:, at] * dot(result_low, d_ref[:, at], 1, 0)).astype(BF16)
            hlow_ref[:, at] = hidden_low
            second = second + dot(hidden_low, u_ref[:, at], 1, 1)
        normed_two, scale_two = norm_parts(mid_ref[...])
        add(0, second * normed_two)
        add(1, second)
        middle_grad = result_grad + norm_back(second, normed_two, scale_two, norm_ref[2:3, :])
        mgrad_ref[...] = middle_grad
        middle_low = middle_grad.astype(BF16)
        mlow_ref[...] = middle_low
        for r in range(n_mp):
            ag_refs[r][...] = dot(middle_low, o_ref[r, :, :cols], 1, 0).astype(BF16)

    row = lambda c: pl.BlockSpec((block, c), lambda i, *_: (i, 0))
    shape = lambda c, t: jax.ShapeDtypeStruct((rows, c), t)
    slots = lambda c: pl.BlockSpec((SLOTS, c), lambda i, *_: (i, 0))
    return pl.pallas_call(
        kernel,
        grid_spec=pltpu.PrefetchScalarGridSpec(
            num_scalar_prefetch=1,
            grid=(rows // block,),
            in_specs=[row(dim), row(dim), row(hidden_size), slots(dim), slots(128), row(1), whole(params.shape)] + [ANY] * 6,
            out_specs=[row(dim), row(hidden_size), row(dim), row(dim)] + [row(cols)] * n_mp + [whole((5, 8, dim))],
            scratch_shapes=[
                pltpu.VMEM((n_mp, dim, out_cols), BF16),
                pltpu.VMEM((dim, hidden_size), BF16),
                pltpu.VMEM((dim, hidden_size), BF16),
                pltpu.SemaphoreType.DMA((blocks_of(oc) + blocks_of(up) + blocks_of(down),)),
            ],
        ),
        out_shape=[shape(dim, BF16), shape(hidden_size, BF16), shape(dim, BF16), shape(dim, F32)]
        + [shape(cols, BF16)] * n_mp
        + [jax.ShapeDtypeStruct((5, 8, dim), F32)],
        compiler_params=PARAMS,
        cost_estimate=cost(2 * rows * dim * (2 * hidden_size + dim), rows * hidden_size * 8),
        name="feed_back",
    )(ids, result, middle, slope, row_grads, stats, seg_col, params, oc[0][0], oc[1][0], up[0][0], up[1][0], down[0][0], down[1][0])


def weight_grad(plan, ids, left, right, name):
    rows, dim = left.shape
    n_mp = plan.n_mp
    parts = right if isinstance(right, list) else None
    width = parts[0].shape[1] if parts else right.shape[1] // n_mp
    out_width = -(-width // 128) * 128
    half = n_mp // 2
    far = plan.groups // 2

    def kernel(ids_ref, left_ref, *refs):
        right_refs, (keep_ref, send_ref) = refs[:-2], refs[-2:]
        me = ids_ref[0]
        step = pl.program_id(0)

        def body(rhs_ref, out_ref):
            grad = dot(left_ref[...], rhs_ref[...], 0, 0).astype(BF16)
            if out_width != width:
                grad = jnp.concatenate([grad, jnp.zeros((dim, out_width - width), BF16)], axis=1)
            for g in range(plan.groups):
                r = g ^ me
                out_ref[r & 1, r >> 1] = grad[g * plan.block : (g + 1) * plan.block]

        for i in range(n_mp):
            out_ref = keep_ref if i < half else send_ref
            if parts:
                rhs_ref = right_refs[i % half * 2 + i // half]
                pl.when(step == i)(functools.partial(body, rhs_ref, out_ref))
        if not parts:
            pl.when(step < half)(lambda: body(right_refs[0], keep_ref))
            pl.when(step >= half)(lambda: body(right_refs[0], send_ref))

    at = lambda i, ids_ref: ids_ref[1] ^ (i % half * 2 + i // half)
    rights = parts or [right]
    if parts:
        right_specs = [whole((rows, width))] * n_mp
    else:
        right_specs = [pl.BlockSpec((rows, width), lambda i, ids_ref: (0, at(i, ids_ref)))]
    out_block = (None, 2, far, plan.block, out_width)
    out = jax.ShapeDtypeStruct((half, 2, far, plan.block, out_width), BF16)
    return pl.pallas_call(
        kernel,
        grid_spec=pltpu.PrefetchScalarGridSpec(
            num_scalar_prefetch=1,
            grid=(n_mp,),
            in_specs=[whole((rows, dim))] + right_specs,
            out_specs=[
                pl.BlockSpec(out_block, lambda i, *_: (jnp.minimum(i, half - 1), 0, 0, 0, 0)),
                pl.BlockSpec(out_block, lambda i, *_: (jnp.maximum(i - half, 0), 0, 0, 0, 0)),
            ],
        ),
        out_shape=[out, out],
        compiler_params=PARAMS,
        cost_estimate=cost(2 * rows * dim * width * n_mp, 2 * dim * width * n_mp),
        name=name,
    )(ids, left, *rights)


def assemble(plan, ids, own, across, mates, dtype, name):
    seqs, share, dim = own.shape
    n_mp = plan.n_mp

    def kernel(ids_ref, own_ref, across_ref, mate_ref, out_ref):
        r = pl.program_id(1)
        value = jnp.where(r == 0, own_ref[...], jnp.where(r == 2, across_ref[...], mate_ref[...]))
        out_ref[...] = value.astype(dtype)

    same = pl.BlockSpec((None, share, dim), lambda s, r, *_: (s, 0, 0))
    return pl.pallas_call(
        kernel,
        grid_spec=pltpu.PrefetchScalarGridSpec(
            num_scalar_prefetch=1,
            grid=(seqs, n_mp),
            in_specs=[same, same, pl.BlockSpec((None, None, share, dim), lambda s, r, *_: (r // 2, s, 0, 0))],
            out_specs=pl.BlockSpec((share, dim), lambda s, r, ids_ref: (s * n_mp + (ids_ref[1] ^ r), 0)),
        ),
        out_shape=jax.ShapeDtypeStruct((seqs * n_mp * share, dim), dtype),
        compiler_params=PARAMS,
        cost_estimate=cost(0, seqs * n_mp * share * dim * 8),
        name=name,
    )(ids, own, across, mates)


def adam_update(weight, moment_one, moment_two, gradient, step_rate, decay_rate):
    fresh_one = BETA_ONE * moment_one + (1.0 - BETA_ONE) * gradient
    fresh_two = BETA_TWO * moment_two + (1.0 - BETA_TWO) * gradient * gradient
    one_hat = fresh_one / (1.0 - BETA_ONE**STEP)
    two_hat = fresh_two / (1.0 - BETA_TWO**STEP)
    updated = weight - step_rate * (one_hat / (jnp.sqrt(two_hat) + ADAM_EPS) + decay_rate * weight)
    return (fresh_one, fresh_two, updated)


def shards(
    tokens,
    seg_ids,
    labels,
    w_qkv,
    m_qkv,
    v_qkv,
    w_out,
    m_out,
    v_out,
    w_up,
    m_up,
    v_up,
    w_down,
    m_down,
    v_down,
    w_cls,
    m_cls,
    v_cls,
    norm_params,
    m_norm,
    v_norm,
    qk_gain,
    m_qk,
    v_qk,
    *,
    n_dp,
    n_mp,
):
    dp, mp = lax.axis_index("dp"), lax.axis_index("mp")
    group_rows, dim = tokens.shape
    plan = Plan(n_dp, n_mp, dim)
    seqs = group_rows // LEN
    share = LEN // n_mp
    rows = seqs * share
    cols = w_qkv.shape[2]
    classes = w_cls.shape[1]
    class_cols = -(-classes // 128) * 128
    out_cols = -(-cols // 128) * 128
    ids = jnp.stack([dp // plan.merge, mp]).astype(jnp.int32)

    qkv_low = plan.merged(w_qkv.astype(BF16), 1)
    qk_pieces = plan.gather(qkv_low[:2], "zy")
    v_pieces = plan.gather(qkv_low[2:], "yz")

    new_image = seg_ids != jnp.concatenate([jnp.full((1,), -1, jnp.int32), seg_ids[:-1]])
    count = jnp.sum((new_image & (seg_ids != PAD_ID)).astype(F32))
    dim_part, head_part = norm_params.shape[1], qk_gain.shape[2]
    small = jnp.zeros((16, dim), F32)
    small = lax.dynamic_update_slice(small, lax.reduce_precision(norm_params, 8, 7), (0, dp * dim_part))
    gain_row = jnp.zeros((2, cols // HEAD, HEAD), F32)
    gain_row = lax.dynamic_update_slice(gain_row, lax.reduce_precision(qk_gain, 8, 7), (0, 0, dp * head_part))
    small = lax.dynamic_update_slice(small, gain_row.reshape(2, cols), (8, 0))
    small = lax.dynamic_update_slice(small, jnp.broadcast_to(count, (1, 1)), (10, 0))
    small = plan.total(small, "dp")
    params, gains, image_total = small[:8], small[8:10, :cols], small[10, 0]

    low_up = plan.merged(w_up.astype(BF16), 0)
    low_down = plan.merged(w_down.T.astype(BF16), 0)
    low_oc = plan.merged(
        jnp.concatenate(
            [
                jnp.pad(w_out.T.astype(BF16), ((0, 0), (0, out_cols - cols))),
                jnp.pad(w_cls.astype(BF16), ((0, 0), (0, class_cols - classes))),
            ],
            axis=1,
        ),
        0,
    )
    oc = plan.both_cores(plan.gather(low_oc, "xyz"))
    up = plan.both_cores(plan.gather(low_up, "zyx"))
    down = plan.both_cores(plan.gather(low_down, "zxy"))

    head_of = jnp.arange(cols) // HEAD
    ones = jnp.where(head_of[:, None] == head_of[None, :], 1.0 / HEAD, 0.0).astype(BF16)
    starts, widths, live = key_windows(seg_ids)
    seg_col = seg_ids.reshape(group_rows, 1)
    seg_row = seg_ids.reshape(-1, 1, LEN)
    normed_low, pq, pk, q, k, v = project(plan, ids, tokens, qk_pieces, v_pieces, params, gains, ones)
    logs, received = [], []
    for s in range(seqs):
        *parts, log = attend(plan, s, ids, starts, widths, q, k, v, seg_col, seg_row)
        logs.append(log)
        received.append([parts[0]] + [plan.swap(parts[r], "mp", r) for r in range(1, n_mp)])
    attended = [jnp.concatenate([received[s][r] for s in range(seqs)], axis=0) for r in range(n_mp)]

    own = lambda a: lax.dynamic_slice_in_dim(a.reshape((seqs, n_mp, share) + a.shape[1:]), mp, 1, 1)
    x = own(tokens).reshape(rows, dim)
    seg = own(seg_ids).reshape(rows)
    middle, second_low, active, slope = feed_up(plan, ids, x, attended, params, oc, up, out_cols)
    result, block_rows, pool = feed_down(plan, ids, middle, active, seg.reshape(seqs, 1, share), params, down)

    def spread(part):
        across = plan.swap(part, "mp", 2)
        return across, plan.swap(jnp.stack([part, across]), "mp", 1)

    block_rows = block_rows.reshape(seqs, share, dim)
    block_across, block_mates = spread(block_rows)
    block_out = assemble(plan, ids, block_rows, block_across, block_mates, BF16, "block_out")

    pool = combine_pools(plan, combine_pools(plan, pool, 1, dim), 2, dim)
    slot_label = labels.reshape(seqs, IMG_SEQ)
    slot_label = slot_label // classes * class_cols + slot_label % classes
    slot_label = jnp.pad(slot_label, ((0, 0), (0, SLOTS - IMG_SEQ)), constant_values=-1).reshape(seqs * SLOTS, 1)
    images = jnp.broadcast_to(image_total, (8, 128))
    row_grads, stats, loss, cls_blocks = classify(plan, ids, pool, slot_label, images, oc, classes, class_cols, out_cols)
    mean_loss = plan.total(loss, "dp")[0, 0] / image_total

    result_low, hidden_low, middle_low, middle_grad, *rest = feed_back(
        plan, ids, result, middle, slope, row_grads, stats, seg.reshape(rows, 1), params, oc, up, down, out_cols, cols
    )
    grads, sums = rest[:n_mp], rest[n_mp]
    grad_parts = [grads[0]] + [plan.swap(grads[r], "mp", r) for r in range(1, n_mp)]
    down_keep, down_send = weight_grad(plan, ids, result_low, active, "grad_down")
    grad_down = plan.scatter(down_keep, down_send, "yxz").T
    up_keep, up_send = weight_grad(plan, ids, second_low, hidden_low, "grad_up")
    grad_up = plan.scatter(up_keep, up_send, "xyz")
    out_keep, out_send = weight_grad(plan, ids, middle_low, attended, "grad_out")
    out_sum = out_keep.astype(F32) + plan.swap(out_send, "mp", 1).astype(F32)
    out_sum = out_sum[0] + plan.swap(out_sum[1].astype(BF16), "mp", 2).astype(F32)
    cls_blocks = cls_blocks.reshape(out_sum.shape[:3] + (class_cols,)).astype(F32)
    both = plan.scatter_rest(jnp.concatenate([out_sum, cls_blocks], axis=3), "yz", "yz", 0)
    grad_out, grad_cls = both[:, :cols].T, both[:, out_cols : out_cols + classes]

    w_grad = None
    norm_one = norm_parts(x.astype(F32))
    first_sums = []
    input_rows, input_across, input_mates = [], [], []
    for s in range(seqs):
        dq, dk, dv = attend_back(plan, s, ids, starts, widths, live, q, k, v, grad_parts, logs[s], seg_col, seg_row)
        keep, send, *w_grad = project_back(
            plan, s, ids, normed_low, pq, pk, dq, dk, dv, w_grad, qk_pieces, v_pieces, gains, ones
        )
        joint = keep.astype(F32) + plan.swap(send, "mp", 1).astype(F32)
        first = joint[0] + plan.swap(joint[1].astype(BF16), "mp", 2).astype(F32)
        at = slice(s * share, (s + 1) * share)
        normed, scale = norm_one[0][at], norm_one[1][at]
        first_sums.append(jnp.stack([jnp.sum(first * normed, axis=0), jnp.sum(first, axis=0)]))
        part = (middle_grad[at] + norm_back(first, normed, scale, params[0:1])).astype(BF16)
        across, mates = spread(part)
        input_rows.append(part)
        input_across.append(across)
        input_mates.append(mates)
    input_grad = assemble(
        plan, ids, jnp.stack(input_rows), jnp.stack(input_across), jnp.stack(input_mates, axis=1), F32, "input_grad"
    )

    grad_w, gain_parts = w_grad
    order = jnp.arange(plan.groups, dtype=jnp.int32)
    order = (order % (plan.groups // 2) * 2 + order // (plan.groups // 2)) ^ ids[0]
    qkv_blocks = jnp.take(grad_w.reshape(3, plan.groups, plan.block, cols), order, axis=1)
    qkv_blocks = qkv_blocks.transpose(1, 0, 2, 3).reshape(2, plan.groups // 2, 3, plan.block, cols)
    grad_qkv = plan.scatter_rest(qkv_blocks, "yz", "yz", 1)

    sums = jnp.sum(sums, axis=1)
    first_sum = sum(first_sums)
    norm_grads = plan.total(jnp.concatenate([first_sum, sums, jnp.zeros((1, dim), F32)], axis=0), "mp")
    qk_grads = jnp.sum(gain_parts, axis=1)
    qk_grads = jnp.pad(qk_grads, ((0, 6), (0, dim - cols)))
    small_grads = plan.total(jnp.concatenate([norm_grads, qk_grads], axis=0), "dp")
    norm_part = lax.dynamic_slice(small_grads, (0, dp * dim_part), (7, dim_part))
    qk_part = lax.dynamic_slice_in_dim(small_grads[8:10, :cols].reshape(2, cols // HEAD, HEAD), dp * head_part, head_part, 2)
    reduced = (grad_qkv, grad_out, grad_up, grad_down, grad_cls, norm_part, qk_part)
    groups = (
        (w_qkv, m_qkv, v_qkv, MATRIX_RATE, MATRIX_DECAY),
        (w_out, m_out, v_out, MATRIX_RATE, MATRIX_DECAY),
        (w_up, m_up, v_up, MATRIX_RATE, MATRIX_DECAY),
        (w_down, m_down, v_down, MATRIX_RATE, MATRIX_DECAY),
        (w_cls, m_cls, v_cls, MATRIX_RATE, MATRIX_DECAY),
        (norm_params, m_norm, v_norm, GAIN_RATE, 0.0),
        (qk_gain, m_qk, v_qk, GAIN_RATE, 0.0),
    )
    outputs = [block_out, input_grad, mean_loss]
    for number, group in enumerate(groups):
        fresh_one, fresh_two, updated = adam_update(group[0], group[1], group[2], reduced[number], group[3], group[4])
        if number == 5:
            outputs = outputs + [fresh_one, fresh_two[:6], fresh_two[6], updated]
        else:
            outputs = outputs + [fresh_one, fresh_two, updated]
    return tuple(outputs)


def solution(mesh):
    rows_cols = (P("mp", "dp"),) * 3
    cols_rows = (P("dp", "mp"),) * 3
    qkv_spec = (P(None, "dp", "mp"),) * 3
    qk_spec = (P(None, "mp", "dp"),) * 3
    norm_spec = P(None, "dp")
    in_specs = (
        (P("dp", None), P("dp"), P("dp")) + qkv_spec + rows_cols + cols_rows + rows_cols + cols_rows + (norm_spec,) * 3 + qk_spec
    )
    out_specs = (
        (P("dp", None), P("dp", None), P())
        + qkv_spec
        + rows_cols
        + cols_rows
        + rows_cols
        + cols_rows
        + (norm_spec, norm_spec, P("dp"), norm_spec)
        + qk_spec
    )
    body = functools.partial(shards, n_dp=mesh.shape["dp"], n_mp=mesh.shape["mp"])
    return jax.shard_map(body, mesh=mesh, in_specs=in_specs, out_specs=out_specs, check_vma=False)
```

time: 1580 us -> 613 us (0.39)
  waiting for transfers between devices: 674 us -> 152 us
  matrix products: 249 us -> 0 us
  Pallas kernels: 0 us -> 232 us
  blocking collectives: 228 us -> 0 us
  local copies, waits for them, and re-layouts: 203 us -> 48 us
  other arithmetic: 190 us -> 63.5 us
  starting transfers between devices: 1.09 us -> 104 us
  between operations: 21.1 us -> 5.05 us
    psum x4 -> x0, waiting for transfers between devices: 447 us -> none  [the longest x1 167 us: shards(): attn_sum = lax.psum(head_terms, 'mp')]
    dot_general x39 -> x0, matrix products: 237 us -> none  [the longest x3 26.7 us: attend_back(): jnp.einsum('hqk,qhe->khe', soft_probs.astype(jnp.bfloat16), grad_slot, pr...]
    pallas_call x0 -> x19, Pallas kernels: none -> 232 us  [the longest x3 43.1 us: project_back(): pl.pallas_call(kernel, grid_spec=pltpu.PrefetchScalarGridSpec(num_scalar_...]
    all_gather x5 -> x0, blocking collectives: 156 us -> none  [the longest x1 35.3 us: shards(): lax.all_gather(w_qkv.astype(jnp.bfloat16), 'dp', axis=1, tiled=True)]
    ppermute x0 -> x87, waiting for transfers between devices: none -> 152 us  [swap(): return lax.ppermute(value, axis, [(i, i ^ bits) for i in range(size)])]
    unnamed x15 -> x0, waiting for transfers between devices: 117 us -> none
    reduce_scatter x3 -> x0, waiting for transfers between devices: 110 us -> none  [the longest x1 69.6 us: shards(): lax.psum_scatter(grad_up, 'dp', scatter_dimension=0, tiled=True)]
    ppermute x0 -> x87, starting transfers between devices: none -> 104 us  [swap(): return lax.ppermute(value, axis, [(i, i ^ bits) for i in range(size)])]
  transfers between devices with their start and end apart: 12 -> 87, of which waited for: 8 -> 34; matrix products, arithmetic and copies ran while one was open for 10% -> 17% of each run, Pallas kernels for 0% -> 35%
where the time goes in v1:
time: 613 us; the launch traced here: 604 us
  Pallas kernels  232 us (38%)
  waiting for transfers between devices  152 us (25%)
  starting transfers between devices  104 us (17%)
  other arithmetic  63.5 us (10%)
  local copies, waits for them, and re-layouts  48 us (8%)
    ppermute x87, waiting for transfers between devices, swap(): return lax.ppermute(value, axis, [(i, i ^ bits) for i in range(size)])  152 us
    ppermute x87, starting transfers between devices, swap(): return lax.ppermute(value, axis, [(i, i ^ bits) for i in range(size)])  104 us
    pallas_call x3, Pallas kernels, project_back(): pl.pallas_call(kernel, grid_spec=pltpu.PrefetchScalarGridSpec(num_scalar_...  43.1 us
    pallas_call x3, Pallas kernels, attend_back(): pl.pallas_call(kernel, grid_spec=pltpu.PrefetchScalarGridSpec(num_scalar_...  33.2 us
    pallas_call x3, Pallas kernels, attend(): pl.pallas_call(kernel, grid_spec=pltpu.PrefetchScalarGridSpec(num_scalar_...  29.1 us
    pallas_call x3, Pallas kernels, weight_grad(): pl.pallas_call(kernel, grid_spec=pltpu.PrefetchScalarGridSpec(num_scalar_...  23.9 us
    pallas_call x1, Pallas kernels, feed_back(): pl.pallas_call(kernel, grid_spec=pltpu.PrefetchScalarGridSpec(num_scalar_...  23.9 us
    pallas_call x2, Pallas kernels, assemble(): pl.pallas_call(kernel, grid_spec=pltpu.PrefetchScalarGridSpec(num_scalar_...  21.4 us
  transfers between devices with their start and end apart: 87, of which 34 were waited for; matrix products, arithmetic and copies ran while one was open for 17% of the time, Pallas kernels for 35%

profile of v1, /device:TPU:0, one launch (start us, length us, event | category | flops | bytes accessed | tf_op | source)
XLA Modules:
  0.0 604.2 jit_solution(1300852962880340329)
XLA Ops:
  1.8 3.1 collective-permute-start.3
  26.4 3.2 collective-permute-done
  29.6 3.7 collective-permute-start.27
  35.7 7.3 %collective-permute-done.1 = f32[16,768]{1,0:T(8,128)S(1)} collective-permute-done((f32[16,768]{1,0:T(8,128)S(1)}, f32[16,768]{1,0:T(8,128)S(1)}, u32[]{:S(2)}, u32[]{:S(2)}) %collective-permute-start.1) | collective-permute-done | bytes 49184 | tf_op jit(solution)/shard_map/ppermute | solution.py:86
  47.5 7.9 %collective-permute-start.9 = (bf16[2,1,96,192]{3,2,1,0:T(8,128)(2,1)S(1)}, bf16[2,1,96,192]{3,2,1,0:T(8,128)(2,1)S(1)}, u32[]{:S(2)}, u32[]{:S(2)}) collective-permute-start(bf16[2,1,96,192]{3,2,1,0:T(8,128)(2,1)S(1)} %pad_maximum_fusion.13), channel_id=1, source_target_pairs={{0,16},{4,20},{8,24},{12,28},{16,0},{20,4},{24,8},{28,12},{1,17},{... | collective-permute-start | bytes 221192 | tf_op jit(solution)/shard_map/ppermute | solution.py:86
  62.6 7.9 %collective-permute-done.29 = bf16[4,96,768]{2,1,0:T(8,128)(2,1)S(1)} collective-permute-done((bf16[4,96,768]{2,1,0:T(8,128)(2,1)S(1)}, bf16[4,96,768]{2,1,0:T(8,128)(2,1)S(1)}, u32[]{:S(2)}, u32[]{:S(2)}) %collective-permute-start.29) | collective-permute-done | bytes 589856 | tf_op jit(solution)/shard_map/ppermute | solution.py:86
  79.2 4.9 collective-permute-start.2
  87.8 17.6 %collective-permute-done.21 = bf16[2,96,512]{2,1,0:T(8,128)(2,1)S(1)} collective-permute-done((bf16[2,96,512]{2,1,0:T(8,128)(2,1)S(1)}, bf16[2,96,512]{2,1,0:T(8,128)(2,1)S(1)}, u32[]{:S(2)}, u32[]{:S(2)}) %collective-permute-start.21) | collective-permute-done | bytes 196640 | tf_op jit(solution)/shard_map/ppermute | solution.py:86
  105.4 5.7 collective-permute-start.22
  111.2 3.7 collective-permute-start.23
  116.3 17.5 %project.1 = (bf16[3072,768]{1,0:T(8,128)(2,1)}, f32[3072,192]{1,0:T(8,128)}, f32[3072,192]{1,0:T(8,128)}, bf16[3072,192]{1,0:T(8,128)(2,1)}, bf16[3072,192]{1,0:T(8,128)(2,1)}, /*index=5*/bf16[3072,192]{1,0:T(8,128)(2,1)}) custom-call(s32[2]{0:T(128)} %pad_add_fusion.ids_ref, bf16[3072,768]{1,0:T(8,128)(2,1)} %x_ref.1, f32[8,768]{1,0:T(8,128)} %slice.302.norm_ref.refs_4_, ...), custom_call_target="tpu_custom_call" | custom-call | flops 2717908992 | bytes 18874368 | tf_op jit(solution)/shard_map/project/pallas_call | solution.py:209
  135.3 5.2 collective-permute-done.23
  140.7 9.6 %attend.4 = (bf16[256,192]{1,0:T(8,128)(2,1)}, bf16[256,192]{1,0:T(8,128)(2,1)}, bf16[256,192]{1,0:T(8,128)(2,1)}, bf16[256,192]{1,0:T(8,128)(2,1)}, f32[1024,128]{1,0:T(8,128)}) custom-call(s32[2]{0:T(128)} %pad_add_fusion.ids_ref, s32[24]{0:T(128)} %select_select_fusion.1.start_ref, s32[24]{0:T(128)} %get-tuple-element.292.width_ref, ...), custom_call_target="tpu_custom_call" | custom-call | flops 805306368 | bytes 1572864 | tf_op jit(solution)/shard_map/attend/pallas_call | solution.py:299
  151.0 9.6 %attend.3 = (bf16[256,192]{1,0:T(8,128)(2,1)}, bf16[256,192]{1,0:T(8,128)(2,1)}, bf16[256,192]{1,0:T(8,128)(2,1)}, bf16[256,192]{1,0:T(8,128)(2,1)}, f32[1024,128]{1,0:T(8,128)}) custom-call(s32[2]{0:T(128)} %pad_add_fusion.ids_ref, s32[24]{0:T(128)} %select_select_fusion.1.start_ref, s32[24]{0:T(128)} %get-tuple-element.292.width_ref, ...), custom_call_target="tpu_custom_call" | custom-call | flops 805306368 | bytes 1572864 | tf_op jit(solution)/shard_map/attend/pallas_call | solution.py:299
  161.8 9.9 %attend.5 = (bf16[256,192]{1,0:T(8,128)(2,1)}, bf16[256,192]{1,0:T(8,128)(2,1)}, bf16[256,192]{1,0:T(8,128)(2,1)}, bf16[256,192]{1,0:T(8,128)(2,1)}, f32[1024,128]{1,0:T(8,128)}) custom-call(s32[2]{0:T(128)} %pad_add_fusion.ids_ref, s32[24]{0:T(128)} %select_select_fusion.1.start_ref, s32[24]{0:T(128)} %get-tuple-element.292.width_ref, ...), custom_call_target="tpu_custom_call" | custom-call | flops 805306368 | bytes 1572864 | tf_op jit(solution)/shard_map/attend/pallas_call | solution.py:299
  173.6 5.2 collective-permute-done.14
  182.1 3.8 collective-permute-done.19
  194.5 16.5 %feed_up.1 = (f32[768,768]{1,0:T(8,128)}, bf16[768,768]{1,0:T(8,128)(2,1)}, bf16[768,3072]{1,0:T(8,128)(2,1)}, f32[768,3072]{1,0:T(8,128)}) custom-call(s32[2]{0:T(128)} %pad_add_fusion.ids_ref, bf16[768,768]{1,0:T(8,128)(2,1)} %bitcast.247, bf16[768,192]{1,0:T(8,128)(2,1)} %copy-done.57, bf16[768,192]{1,0:T(8,128)(2,1)} %copy-done.54, ...), custom_call_target="tpu_custom_call" | custom-call | flops 4529848320 | bytes 18874368 | tf_op jit(solution)/shard_map/feed_up/pallas_call | solution.py:564
  212.6 17.8 %feed_down.1 = (f32[768,768]{1,0:T(8,128)}, bf16[768,768]{1,0:T(8,128)(2,1)}, f32[192,896]{1,0:T(8,128)}) custom-call(s32[2]{0:T(128)} %pad_add_fusion.ids_ref, f32[768,768]{1,0:T(8,128)} %get-tuple-element.108.mid_ref, bf16[768,3072]{1,0:T(8,128)(2,1)} %get-tuple-element.109.act_ref.refs_0_, s32[3,1,256]{2,1,0:T(1,128)} %constant_dynamic-slice_fusion.seg_ref, ...), custom_call_target="tpu_custom_call" | custom-call | flops 3623878656 | bytes 9437184 | tf_op jit(solution)/shard_map/feed_down/pallas_call | solution.py:629
  242.5 12.0 %collective-permute-done.41 = f32[192,896]{1,0:T(8,128)} collective-permute-done((f32[192,896]{1,0:T(8,128)}, f32[192,896]{1,0:T(8,128)}, u32[]{:S(2)}, u32[]{:S(2)}) %collective-permute-start.41) | collective-permute-done | bytes 688160 | tf_op jit(solution)/shard_map/ppermute | solution.py:86
  258.3 5.2 classify.1
  263.6 23.9 %feed_back.1 = (bf16[768,768]{1,0:T(8,128)(2,1)}, bf16[768,3072]{1,0:T(8,128)(2,1)}, bf16[768,768]{1,0:T(8,128)(2,1)}, f32[768,768]{1,0:T(8,128)}, bf16[768,192]...) custom-call(s32[2]{0:T(128)} %pad_add_fusion.ids_ref, ...), custom_call_target="tpu_custom_call" | custom-call | flops 8153726976 | bytes 18874368 | tf_op jit(solution)/shard_map/feed_back/pallas_call | solution.py:803
  295.1 3.3 pad_maximum_fusion
  299.8 7.5 %collective-permute-done.44.refs_3_ = bf16[768,192]{1,0:T(8,128)(2,1)} collective-permute-done((bf16[768,192]{1,0:T(8,128)(2,1)}, bf16[768,192]{1,0:T(8,128)(2,1)}, u32[]{:S(2)}, u32[]{:S(2)}) %collective-permute-start.44) | collective-permute-done | bytes 294944 | tf_op jit(solution)/shard_map/ppermute | solution.py:86
  307.4 10.5 %attend_back.3 = (f32[1024,192]{1,0:T(8,128)}, f32[1024,192]{1,0:T(8,128)}, f32[1024,192]{1,0:T(8,128)}) custom-call(s32[2]{0:T(128)} %pad_add_fusion.ids_ref, s32[24]{0:T(128)} %select_select_fusion.1.start_ref, s32[24]{0:T(128)} %get-tuple-element.292.width_ref, s32[24]{0:T(128)} %reshape.307.live_ref, bf16[3072,192]{1,0:T(8,128)(2,1)} %get-tuple-element.93.q_ref, ...), custom_call_target="tpu_custom_call" | custom-call | flops 2013265920 | bytes 4718592 | tf_op jit(solution)/shard_map/attend_back/pallas_call | solution.py:370
  317.9 13.8 %project_back.3 = (bf16[2,256,768]{2,1,0:T(8,128)(2,1)}, bf16[2,256,768]{2,1,0:T(8,128)(2,1)}, f32[3,768,192]{2,1,0:T(8,128)}, f32[2,8,192]{2,1,0:T(8,128)}) custom-call(s32[2]{0:T(128)} %pad_add_fusion.ids_ref, bf16[3072,768]{1,0:T(8,128)(2,1)} %get-tuple-element.117.low_ref, f32[3072,192]{1,0:T(8,128)} %get-tuple-element.118.pq_ref, ...), custom_call_target="tpu_custom_call" | custom-call | flops 1811939328 | bytes 9437184 | tf_op jit(solution)/shard_map/project_back/pallas_call | solution.py:474
  331.6 11.8 %attend_back.4 = (f32[1024,192]{1,0:T(8,128)}, f32[1024,192]{1,0:T(8,128)}, f32[1024,192]{1,0:T(8,128)}) custom-call(s32[2]{0:T(128)} %pad_add_fusion.ids_ref, s32[24]{0:T(128)} %select_select_fusion.1.start_ref, s32[24]{0:T(128)} %get-tuple-element.292.width_ref, s32[24]{0:T(128)} %reshape.307.live_ref, bf16[3072,192]{1,0:T(8,128)(2,1)} %get-tuple-element.93.q_ref, ...), custom_call_target="tpu_custom_call" | custom-call | flops 2013265920 | bytes 4718592 | tf_op jit(solution)/shard_map/attend_back/pallas_call | solution.py:370
  343.5 14.6 %project_back.4 = (bf16[2,256,768]{2,1,0:T(8,128)(2,1)}, bf16[2,256,768]{2,1,0:T(8,128)(2,1)}, f32[3,768,192]{2,1,0:T(8,128)}, f32[2,8,192]{2,1,0:T(8,128)}) custom-call(s32[2]{0:T(128)} %pad_add_fusion.ids_ref, bf16[3072,768]{1,0:T(8,128)(2,1)} %get-tuple-element.117.low_ref, f32[3072,192]{1,0:T(8,128)} %get-tuple-element.118.pq_ref, ...), custom_call_target="tpu_custom_call" | custom-call | flops 1811939328 | bytes 9437184 | tf_op jit(solution)/shard_map/project_back/pallas_call | solution.py:474
  358.1 10.8 %attend_back.5 = (f32[1024,192]{1,0:T(8,128)}, f32[1024,192]{1,0:T(8,128)}, f32[1024,192]{1,0:T(8,128)}) custom-call(s32[2]{0:T(128)} %pad_add_fusion.ids_ref, s32[24]{0:T(128)} %select_select_fusion.1.start_ref, s32[24]{0:T(128)} %get-tuple-element.292.width_ref, s32[24]{0:T(128)} %reshape.307.live_ref, bf16[3072,192]{1,0:T(8,128)(2,1)} %get-tuple-element.93.q_ref, ...), custom_call_target="tpu_custom_call" | custom-call | flops 2013265920 | bytes 4718592 | tf_op jit(solution)/shard_map/attend_back/pallas_call | solution.py:370
  368.9 14.8 %project_back.5 = (bf16[2,256,768]{2,1,0:T(8,128)(2,1)}, bf16[2,256,768]{2,1,0:T(8,128)(2,1)}, f32[3,768,192]{2,1,0:T(8,128)}, f32[2,8,192]{2,1,0:T(8,128)}) custom-call(s32[2]{0:T(128)} %pad_add_fusion.ids_ref, bf16[3072,768]{1,0:T(8,128)(2,1)} %get-tuple-element.117.low_ref, f32[3072,192]{1,0:T(8,128)} %get-tuple-element.118.pq_ref, ...), custom_call_target="tpu_custom_call" | custom-call | flops 1811939328 | bytes 9437184 | tf_op jit(solution)/shard_map/project_back/pallas_call | solution.py:474
  383.7 3.9 gather_fusion
  391.9 9.0 %grad_down.1 = (bf16[2,2,4,96,768]{4,3,2,1,0:T(8,128)(2,1)}, bf16[2,2,4,96,768]{4,3,2,1,0:T(8,128)(2,1)}) custom-call(s32[2]{0:T(128)} %pad_add_fusion.ids_ref, bf16[768,768]{1,0:T(8,128)(2,1)} %get-tuple-element.156.left_ref, bf16[768,3072]{1,0:T(8,128)(2,1)} %get-tuple-element.109.act_ref.refs_0_), custom_call_target="tpu_custom_call" | custom-call | flops 3623878656 | bytes 4718592 | tf_op jit(solution)/shard_map/grad_down/pallas_call | solution.py:865
  401.2 5.7 collective-permute-start.58
  406.8 5.7 grad_out.1
  414.0 9.2 %grad_up.1 = (bf16[2,2,4,96,768]{4,3,2,1,0:T(8,128)(2,1)}, bf16[2,2,4,96,768]{4,3,2,1,0:T(8,128)(2,1)}) custom-call(s32[2]{0:T(128)} %pad_add_fusion.ids_ref, bf16[768,768]{1,0:T(8,128)(2,1)} %get-tuple-element.152.left_ref, bf16[768,3072]{1,0:T(8,128)(2,1)} %get-tuple-element.153.refs_0_), custom_call_target="tpu_custom_call" | custom-call | flops 3623878656 | bytes 4718592 | tf_op jit(solution)/shard_map/grad_up/pallas_call | solution.py:865
  436.7 7.6 %collective-permute-done.62 = bf16[3,96,192]{2,1,0:T(8,128)(2,1)S(1)} collective-permute-done((bf16[3,96,192]{2,1,0:T(8,128)(2,1)S(1)}, bf16[3,96,192]{2,1,0:T(8,128)(2,1)S(1)}, u32[]{:S(2)}, u32[]{:S(2)}) %collective-permute-start.62) | collective-permute-done | bytes 110624 | tf_op jit(solution)/shard_map/ppermute | solution.py:86
  450.8 7.1 %collective-permute-done.65 = bf16[2,4,96,256]{3,2,1,0:T(8,128)(2,1)S(1)} collective-permute-done((bf16[2,4,96,256]{3,2,1,0:T(8,128)(2,1)S(1)}, bf16[2,4,96,256]{3,2,1,0:T(8,128)(2,1)S(1)}, u32[]{:S(2)}, u32[]{:S(2)}) %collective-permute-start.65) | collective-permute-done | bytes 393248 | tf_op jit(solution)/shard_map/ppermute | solution.py:86
  458.4 7.9 %collective-permute-done.48 = bf16[256,768]{1,0:T(8,128)(2,1)S(1)} collective-permute-done((bf16[256,768]{1,0:T(8,128)(2,1)S(1)}, bf16[256,768]{1,0:T(8,128)(2,1)S(1)}, u32[]{:S(2)}, u32[]{:S(2)}) %collective-permute-start.48) | collective-permute-done | bytes 393248 | tf_op jit(solution)/shard_map/ppermute | solution.py:86
  467.2 7.6 %collective-permute-done.50 = bf16[256,768]{1,0:T(8,128)(2,1)S(1)} collective-permute-done((bf16[256,768]{1,0:T(8,128)(2,1)S(1)}, bf16[256,768]{1,0:T(8,128)(2,1)S(1)}, u32[]{:S(2)}, u32[]{:S(2)}) %collective-permute-start.50) | collective-permute-done | bytes 393248 | tf_op jit(solution)/shard_map/ppermute | solution.py:86
  474.7 7.6 %collective-permute-done.46 = bf16[256,768]{1,0:T(8,128)(2,1)S(1)} collective-permute-done((bf16[256,768]{1,0:T(8,128)(2,1)S(1)}, bf16[256,768]{1,0:T(8,128)(2,1)S(1)}, u32[]{:S(2)}, u32[]{:S(2)}) %collective-permute-start.46) | collective-permute-done | bytes 393248 | tf_op jit(solution)/shard_map/ppermute | solution.py:86
  486.7 3.2 collective-permute-done.83
  491.0 3.1 collective-permute-done.84
  539.1 10.1 %block_out.1 = bf16[3072,768]{1,0:T(8,128)(2,1)} custom-call(s32[2]{0:T(128)} %pad_add_fusion.ids_ref, bf16[3,256,768]{2,1,0:T(8,128)(2,1)} %bitcast.15.own_ref, bf16[3,256,768]{2,1,0:T(8,128)(2,1)} %copy-done.9, bf16[2,3,256,768]{3,2,1,0:T(8,128)(2,1)} %collective-permute-done.39.mate_ref), custom_call_target="tpu_custom_call" | custom-call | bytes 18874368 | tf_op jit(solution)/shard_map/block_out/pallas_call | solution.py:893
  555.6 4.4 collective-permute-done.71
  562.6 3.1 pad_maximum_fusion.1.mate_ref
  565.6 11.3 %input_grad.1 = f32[3072,768]{1,0:T(8,128)} custom-call(s32[2]{0:T(128)} %pad_add_fusion.ids_ref, bf16[3,256,768]{2,1,0:T(8,128)(2,1)} %pad_maximum_fusion.2.own_ref, bf16[3,256,768]{2,1,0:T(8,128)(2,1)} %pad_maximum_fusion.3.across_ref, bf16[2,3,256,768]{3,2,1,0:T(8,128)(2,1)} %pad_maximum_fusion.1.mate_ref), custom_call_target="tpu_custom_call" | custom-call | bytes 18874368 | tf_op jit(solution)/shard_map/input_grad/pallas_call | solution.py:893
  589.0 3.5 collective-permute-done.80
  593.6 8.1 %collective-permute-done.74 = bf16[96,768]{1,0:T(8,128)(2,1)S(1)} collective-permute-done((bf16[96,768]{1,0:T(8,128)(2,1)S(1)}, bf16[96,768]{1,0:T(8,128)(2,1)S(1)}, u32[]{:S(2)}, u32[]{:S(2)}) %collective-permute-start.74) | collective-permute-done | bytes 147488 | tf_op jit(solution)/shard_map/ppermute | solution.py:86
  (516 shorter events, 192.9 us)
Async XLA Ops:
  1.8 31.5 %collective-permute-start.3 = (bf16[1,2,96,192]{3,2,1,0:T(8,128)(2,1)S(1)}, bf16[1,2,96,192]{3,2,1,0:T(8,128)(2,1)S(1)}, u32[]{:S(2)}, u32[]{:S(2)}) collective-permute-start(bf16[1,2,96,192]{3,2,1,0:T(8,128)(2,1)S(1)} %slice_bitcast_fusion.25), channel_id=1, source_target_pairs={{0,8},{4,12},{8,0},{12,4},{16,24},{20,28},{24,16},{28,20},{1,9},{5... | collective-permute-start | bytes 221192 | tf_op jit(solution)/shard_map/ppermute | solution.py:86
  4.9 28.9 %collective-permute-start.4 = (bf16[1,2,96,192]{3,2,1,0:T(8,128)(2,1)S(1)}, bf16[1,2,96,192]{3,2,1,0:T(8,128)(2,1)S(1)}, u32[]{:S(2)}, u32[]{:S(2)}) collective-permute-start(bf16[1,2,96,192]{3,2,1,0:T(8,128)(2,1)S(1)} %slice_bitcast_fusion.25), channel_id=1, source_target_pairs={{0,16},{4,20},{8,24},{12,28},{16,0},{20,4},{24,8},{28,12},{1,17},{... | collective-permute-start | bytes 221192 | tf_op jit(solution)/shard_map/ppermute | solution.py:86
  7.5 27.9 %collective-permute-start.5 = (bf16[1,2,96,192]{3,2,1,0:T(8,128)(2,1)S(1)}, bf16[1,2,96,192]{3,2,1,0:T(8,128)(2,1)S(1)}, u32[]{:S(2)}, u32[]{:S(2)}) collective-permute-start(bf16[1,2,96,192]{3,2,1,0:T(8,128)(2,1)S(1)} %slice_bitcast_fusion.25), channel_id=1, source_target_pairs={{0,24},{4,28},{8,16},{12,20},{16,8},{20,12},{24,0},{28,4},{1,25},{... | collective-permute-start | bytes 221192 | tf_op jit(solution)/shard_map/ppermute | solution.py:86
  7.5 17.9 %collective-permute-start.7 = (bf16[1,1,96,192]{3,2,1,0:T(8,128)(2,1)S(1)}, bf16[1,1,96,192]{3,2,1,0:T(8,128)(2,1)S(1)}, u32[]{:S(2)}, u32[]{:S(2)}) collective-permute-start(bf16[1,1,96,192]{3,2,1,0:T(8,128)(2,1)S(1)} %slice_bitcast_fusion.26), channel_id=1, source_target_pairs={{0,4},{4,0},{8,12},{12,8},{16,20},{20,16},{24,28},{28,24},{1,5},{5... | collective-permute-start | bytes 110600 | tf_op jit(solution)/shard_map/ppermute | solution.py:86
  10.9 34.1 %collective-permute-start.26 = (bf16[1,96,768]{2,1,0:T(8,128)(2,1)S(1)}, bf16[1,96,768]{2,1,0:T(8,128)(2,1)S(1)}, u32[]{:S(2)}, u32[]{:S(2)}) collective-permute-start(bf16[1,96,768]{2,1,0:T(8,128)(2,1)S(1)} %get-tuple-element.291), channel_id=1, source_target_pairs={{0,8},{4,12},{8,0},{12,4},{16,24},{20,28},{24,16},{28,20},{1,9},{5... | collective-permute-start | bytes 442376 | tf_op jit(solution)/shard_map/ppermute | solution.py:86
  29.6 17.8 %collective-permute-start.27 = (bf16[1,96,768]{2,1,0:T(8,128)(2,1)S(1)}, bf16[1,96,768]{2,1,0:T(8,128)(2,1)S(1)}, u32[]{:S(2)}, u32[]{:S(2)}) collective-permute-start(bf16[1,96,768]{2,1,0:T(8,128)(2,1)S(1)} %get-tuple-element.291), channel_id=1, source_target_pairs={{0,16},{4,20},{8,24},{12,28},{16,0},{20,4},{24,8},{28,12},{1,17},{... | collective-permute-start | bytes 442376 | tf_op jit(solution)/shard_map/ppermute | solution.py:86
  42.9 14.6 %collective-permute-start.33 = (bf16[1,96,768]{2,1,0:T(8,128)(2,1)S(1)}, bf16[1,96,768]{2,1,0:T(8,128)(2,1)S(1)}, u32[]{:S(2)}, u32[]{:S(2)}) collective-permute-start(bf16[1,96,768]{2,1,0:T(8,128)(2,1)S(1)} %get-tuple-element.289), channel_id=1, source_target_pairs={{0,16},{4,20},{8,24},{12,28},{16,0},{20,4},{24,8},{28,12},{1,17},{... | collective-permute-start | bytes 442376 | tf_op jit(solution)/shard_map/ppermute | solution.py:86
  47.4 29.6 %collective-permute-start.8 = (bf16[2,1,96,192]{3,2,1,0:T(8,128)(2,1)S(1)}, bf16[2,1,96,192]{3,2,1,0:T(8,128)(2,1)S(1)}, u32[]{:S(2)}, u32[]{:S(2)}) collective-permute-start(bf16[2,1,96,192]{3,2,1,0:T(8,128)(2,1)S(1)} %pad_maximum_fusion.13), channel_id=1, source_target_pairs={{0,8},{4,12},{8,0},{12,4},{16,24},{20,28},{24,16},{28,20},{1,9},{5... | collective-permute-start | bytes 221192 | tf_op jit(solution)/shard_map/ppermute | solution.py:86
  47.5 30.7 %collective-permute-start.9 = (bf16[2,1,96,192]{3,2,1,0:T(8,128)(2,1)S(1)}, bf16[2,1,96,192]{3,2,1,0:T(8,128)(2,1)S(1)}, u32[]{:S(2)}, u32[]{:S(2)}) collective-permute-start(bf16[2,1,96,192]{3,2,1,0:T(8,128)(2,1)S(1)} %pad_maximum_fusion.13), channel_id=1, source_target_pairs={{0,16},{4,20},{8,24},{12,28},{16,0},{20,4},{24,8},{28,12},{1,17},{... | collective-permute-start | bytes 221192 | tf_op jit(solution)/shard_map/ppermute | solution.py:86
  55.4 23.7 %collective-permute-start.10 = (bf16[2,1,96,192]{3,2,1,0:T(8,128)(2,1)S(1)}, bf16[2,1,96,192]{3,2,1,0:T(8,128)(2,1)S(1)}, u32[]{:S(2)}, u32[]{:S(2)}) collective-permute-start(bf16[2,1,96,192]{3,2,1,0:T(8,128)(2,1)S(1)} %pad_maximum_fusion.13), channel_id=1, source_target_pairs={{0,24},{4,28},{8,16},{12,20},{16,8},{20,12},{24,0},{28,4},{1,25},{... | collective-permute-start | bytes 221192 | tf_op jit(solution)/shard_map/ppermute | solution.py:86
  58.3 16.8 %collective-permute-start.35 = (bf16[4,96,768]{2,1,0:T(8,128)(2,1)S(1)}, bf16[4,96,768]{2,1,0:T(8,128)(2,1)S(1)}, u32[]{:S(2)}, u32[]{:S(2)}) collective-permute-start(bf16[4,96,768]{2,1,0:T(8,128)(2,1)S(1)} %pad_maximum_fusion.9), channel_id=1, source_target_pairs={{0,2},{1,3},{2,0},{3,1},{4,6},{5,7},{6,4},{7,5},{8,10},{9,11},{10,... | collective-permute-start | bytes 1769480 | tf_op jit(solution)/shard_map/ppermute | solution.py:86
  71.4 43.6 %collective-permute-start.30 = (bf16[8,96,768]{2,1,0:T(8,128)(2,1)S(1)}, bf16[8,96,768]{2,1,0:T(8,128)(2,1)S(1)}, u32[]{:S(2)}, u32[]{:S(2)}) collective-permute-start(bf16[8,96,768]{2,1,0:T(8,128)(2,1)S(1)} %get-tuple-element.314), channel_id=1, source_target_pairs={{0,2},{1,3},{2,0},{3,1},{4,6},{5,7},{6,4},{7,5},{8,10},{9,11},{10,... | collective-permute-start | bytes 3538952 | tf_op jit(solution)/shard_map/ppermute | solution.py:86
  76.1 57.6 %collective-permute-start.36 = (bf16[8,96,768]{2,1,0:T(8,128)(2,1)S(1)}, bf16[8,96,768]{2,1,0:T(8,128)(2,1)S(1)}, u32[]{:S(2)}, u32[]{:S(2)}) collective-permute-start(bf16[8,96,768]{2,1,0:T(8,128)(2,1)S(1)} %get-tuple-element.312), channel_id=1, source_target_pairs={{0,4},{4,0},{8,12},{12,8},{16,20},{20,16},{24,28},{28,24},{1,5},{5... | collective-permute-start | bytes 3538952 | tf_op jit(solution)/shard_map/ppermute | solution.py:86
  77.0 37.9 %collective-permute-start.6 = (bf16[4,2,96,192]{3,2,1,0:T(8,128)(2,1)S(1)}, bf16[4,2,96,192]{3,2,1,0:T(8,128)(2,1)S(1)}, u32[]{:S(2)}, u32[]{:S(2)}) collective-permute-start(bf16[4,2,96,192]{3,2,1,0:T(8,128)(2,1)S(1)} %pad_maximum_fusion.10), channel_id=1, source_target_pairs={{0,4},{4,0},{8,12},{12,8},{16,20},{20,16},{24,28},{28,24},{1,5},{5... | collective-permute-start | bytes 884744 | tf_op jit(solution)/shard_map/ppermute | solution.py:86
  78.2 27.2 %collective-permute-start.21 = (bf16[2,96,512]{2,1,0:T(8,128)(2,1)S(1)}, bf16[2,96,512]{2,1,0:T(8,128)(2,1)S(1)}, u32[]{:S(2)}, u32[]{:S(2)}) collective-permute-start(bf16[2,96,512]{2,1,0:T(8,128)(2,1)S(1)} %pad_maximum_fusion.12), channel_id=1, source_target_pairs={{0,4},{4,0},{8,12},{12,8},{16,20},{20,16},{24,28},{28,24},{1,5},{5... | collective-permute-start | bytes 589832 | tf_op jit(solution)/shard_map/ppermute | solution.py:86
  105.4 29.9 %collective-permute-start.22 = (bf16[4,96,512]{2,1,0:T(8,128)(2,1)S(1)}, bf16[4,96,512]{2,1,0:T(8,128)(2,1)S(1)}, u32[]{:S(2)}, u32[]{:S(2)}) collective-permute-start(bf16[4,96,512]{2,1,0:T(8,128)(2,1)S(1)} %pad_maximum_fusion.11), channel_id=1, source_target_pairs={{0,8},{4,12},{8,0},{12,4},{16,24},{20,28},{24,16},{28,20},{1,9},{5... | collective-permute-start | bytes 1179656 | tf_op jit(solution)/shard_map/ppermute | solution.py:86
  111.2 29.4 %collective-permute-start.23 = (bf16[4,96,512]{2,1,0:T(8,128)(2,1)S(1)}, bf16[4,96,512]{2,1,0:T(8,128)(2,1)S(1)}, u32[]{:S(2)}, u32[]{:S(2)}) collective-permute-start(bf16[4,96,512]{2,1,0:T(8,128)(2,1)S(1)} %pad_maximum_fusion.11), channel_id=1, source_target_pairs={{0,16},{4,20},{8,24},{12,28},{16,0},{20,4},{24,8},{28,12},{1,17},{... | collective-permute-start | bytes 1179656 | tf_op jit(solution)/shard_map/ppermute | solution.py:86
  114.9 25.7 %collective-permute-start.24 = (bf16[4,96,512]{2,1,0:T(8,128)(2,1)S(1)}, bf16[4,96,512]{2,1,0:T(8,128)(2,1)S(1)}, u32[]{:S(2)}, u32[]{:S(2)}) collective-permute-start(bf16[4,96,512]{2,1,0:T(8,128)(2,1)S(1)} %pad_maximum_fusion.11), channel_id=1, source_target_pairs={{0,24},{4,28},{8,16},{12,20},{16,8},{20,12},{24,0},{28,4},{1,25},{... | collective-permute-start | bytes 1179656 | tf_op jit(solution)/shard_map/ppermute | solution.py:86
  116.2 77.1 %collective-permute-start.31 = (bf16[16,96,768]{2,1,0:T(8,128)(2,1)}, bf16[16,96,768]{2,1,0:T(8,128)(2,1)}, u32[]{:S(2)}, u32[]{:S(2)}) collective-permute-start(bf16[16,96,768]{2,1,0:T(8,128)(2,1)} %constant_dynamic-update-slice_fusion.33.refs_7_.u_a), channel_id=1, source_target_pairs={{0,1},{1,0},{2,3},{3,2},{4,5},{5,4},{6,7},{7,6},{8,9},{9,8},{10,11... | collective-permute-start | bytes 7077896 | tf_op jit(solution)/shard_map/ppermute | solution.py:86
  134.8 76.2 %collective-permute-start.37 = (bf16[16,96,768]{2,1,0:T(8,128)(2,1)}, bf16[16,96,768]{2,1,0:T(8,128)(2,1)S(1)}, u32[]{:S(2)}, u32[]{:S(2)}) collective-permute-start(bf16[16,96,768]{2,1,0:T(8,128)(2,1)} %constant_dynamic-update-slice_fusion.44.d_a), channel_id=1, source_target_pairs={{0,1},{1,0},{2,3},{3,2},{4,5},{5,4},{6,7},{7,6},{8,9},{9,8},{10,11... | collective-permute-start | bytes 7077896 | tf_op jit(solution)/shard_map/ppermute | solution.py:86
  140.6 52.6 %collective-permute-start.25 = (bf16[16,96,512]{2,1,0:T(8,128)(2,1)S(1)}, bf16[16,96,512]{2,1,0:T(8,128)(2,1)S(1)}, u32[]{:S(2)}, u32[]{:S(2)}) collective-permute-start(bf16[16,96,512]{2,1,0:T(8,128)(2,1)S(1)} %constant_dynamic-update-slice_fusion.22.refs_5_.c_a.oc_a), channel_id=1, source_target_pairs={{0,1},{1,0},{2,3},{3,2},{4,5},{5,4},{6,7},{7,6},{8,9},{9,8},{10,11... | collective-permute-start | bytes 4718600 | tf_op jit(solution)/shard_map/ppermute | solution.py:86
  150.3 30.2 %collective-permute-start.18 = (bf16[256,192]{1,0:T(8,128)(2,1)}, bf16[256,192]{1,0:T(8,128)(2,1)S(1)}, u32[]{:S(2)}, u32[]{:S(2)}) collective-permute-start(bf16[256,192]{1,0:T(8,128)(2,1)} %get-tuple-element.106), channel_id=1, source_target_pairs={{0,3},{1,2},{2,1},{3,0},{4,7},{5,6},{6,5},{7,4},{8,11},{9,10},{10,... | collective-permute-start | bytes 294920 | tf_op jit(solution)/shard_map/ppermute | solution.py:86
  235.9 18.6 %collective-permute-start.41 = (f32[192,896]{1,0:T(8,128)}, f32[192,896]{1,0:T(8,128)}, u32[]{:S(2)}, u32[]{:S(2)}) collective-permute-start(f32[192,896]{1,0:T(8,128)} %maximum_maximum_fusion), channel_id=1, source_target_pairs={{0,2},{1,3},{2,0},{3,1},{4,6},{5,7},{6,4},{7,5},{8,10},{9,11},{10,... | collective-permute-start | bytes 2064392 | tf_op jit(solution)/shard_map/ppermute | solution.py:86
  241.0 54.1 %collective-permute-start.38 = (bf16[3,256,768]{2,1,0:T(8,128)(2,1)}, bf16[3,256,768]{2,1,0:T(8,128)(2,1)S(1)}, u32[]{:S(2)}, u32[]{:S(2)}) collective-permute-start(bf16[3,256,768]{2,1,0:T(8,128)(2,1)} %bitcast.15.own_ref), channel_id=1, source_target_pairs={{0,2},{1,3},{2,0},{3,1},{4,6},{5,7},{6,4},{7,5},{8,10},{9,11},{10,... | collective-permute-start | bytes 3538952 | tf_op jit(solution)/shard_map/ppermute | solution.py:86
  288.1 19.2 %collective-permute-start.44 = (bf16[768,192]{1,0:T(8,128)(2,1)}, bf16[768,192]{1,0:T(8,128)(2,1)}, u32[]{:S(2)}, u32[]{:S(2)}) collective-permute-start(bf16[768,192]{1,0:T(8,128)(2,1)} %get-tuple-element.124), channel_id=1, source_target_pairs={{0,3},{1,2},{2,1},{3,0},{4,7},{5,6},{6,5},{7,4},{8,11},{9,10},{10,... | collective-permute-start | bytes 884744 | tf_op jit(solution)/shard_map/ppermute | solution.py:86
  298.5 102.7 %collective-permute-start.57 = (f32[8,128]{1,0:T(8,128)S(1)}, f32[8,128]{1,0:T(8,128)S(1)}, u32[]{:S(2)}, u32[]{:S(2)}) collective-permute-start(f32[8,128]{1,0:T(8,128)S(1)} %copy-done.69), channel_id=1, source_target_pairs={{0,4},{4,0},{8,12},{12,8},{16,20},{20,16},{24,28},{28,24},{1,5},{5... | collective-permute-start | bytes 12296 | tf_op jit(solution)/shard_map/ppermute | solution.py:86
  391.9 34.8 %collective-permute-start.60 = (bf16[4,3,96,192]{3,2,1,0:T(8,128)(2,1)}, bf16[4,3,96,192]{3,2,1,0:T(8,128)(2,1)}, u32[]{:S(2)}, u32[]{:S(2)}) collective-permute-start(bf16[4,3,96,192]{3,2,1,0:T(8,128)(2,1)} %slice.584), channel_id=1, source_target_pairs={{0,4},{4,0},{8,12},{12,8},{16,20},{20,16},{24,28},{28,24},{1,5},{5... | collective-permute-start | bytes 1327112 | tf_op jit(solution)/shard_map/ppermute | solution.py:86
  400.9 119.2 %collective-permute-start.76 = (bf16[2,2,4,96,768]{4,3,2,1,0:T(8,128)(2,1)}, bf16[2,2,4,96,768]{4,3,2,1,0:T(8,128)(2,1)}, u32[]{:S(2)}, u32[]{:S(2)}) collective-permute-start(bf16[2,2,4,96,768]{4,3,2,1,0:T(8,128)(2,1)} %get-tuple-element.158), channel_id=1, source_target_pairs={{0,1},{1,0},{2,3},{3,2},{4,5},{5,4},{6,7},{7,6},{8,9},{9,8},{10,11... | collective-permute-start | bytes 7077896 | tf_op jit(solution)/shard_map/ppermute | solution.py:86
  412.5 18.1 %collective-permute-start.64 = (bf16[2,2,4,96,256]{4,3,2,1,0:T(8,128)(2,1)}, bf16[2,2,4,96,256]{4,3,2,1,0:T(8,128)(2,1)}, u32[]{:S(2)}, u32[]{:S(2)}) collective-permute-start(bf16[2,2,4,96,256]{4,3,2,1,0:T(8,128)(2,1)} %get-tuple-element.150), channel_id=1, source_target_pairs={{0,1},{1,0},{2,3},{3,2},{4,5},{5,4},{6,7},{7,6},{8,9},{9,8},{10,11... | collective-permute-start | bytes 2359304 | tf_op jit(solution)/shard_map/ppermute | solution.py:86
  425.9 20.1 %collective-permute-start.47 = (bf16[2,256,768]{2,1,0:T(8,128)(2,1)}, bf16[2,256,768]{2,1,0:T(8,128)(2,1)}, u32[]{:S(2)}, u32[]{:S(2)}) collective-permute-start(bf16[2,256,768]{2,1,0:T(8,128)(2,1)} %get-tuple-element.137), channel_id=1, source_target_pairs={{0,1},{1,0},{2,3},{3,2},{4,5},{5,4},{6,7},{7,6},{8,9},{9,8},{10,11... | collective-permute-start | bytes 2359304 | tf_op jit(solution)/shard_map/ppermute | solution.py:86
  436.7 89.3 %collective-permute-start.70 = (bf16[2,2,4,96,768]{4,3,2,1,0:T(8,128)(2,1)}, bf16[2,2,4,96,768]{4,3,2,1,0:T(8,128)(2,1)}, u32[]{:S(2)}, u32[]{:S(2)}) collective-permute-start(bf16[2,2,4,96,768]{4,3,2,1,0:T(8,128)(2,1)} %get-tuple-element.155), channel_id=1, source_target_pairs={{0,1},{1,0},{2,3},{3,2},{4,5},{5,4},{6,7},{7,6},{8,9},{9,8},{10,11... | collective-permute-start | bytes 7077896 | tf_op jit(solution)/shard_map/ppermute | solution.py:86
  447.7 18.7 %collective-permute-start.48 = (bf16[256,768]{1,0:T(8,128)(2,1)S(1)}, bf16[256,768]{1,0:T(8,128)(2,1)S(1)}, u32[]{:S(2)}, u32[]{:S(2)}) collective-permute-start(bf16[256,768]{1,0:T(8,128)(2,1)S(1)} %fusion.21), channel_id=1, source_target_pairs={{0,2},{1,3},{2,0},{3,1},{4,6},{5,7},{6,4},{7,5},{8,10},{9,11},{10,... | collective-permute-start | bytes 1179656 | tf_op jit(solution)/shard_map/ppermute | solution.py:86
  449.7 25.0 %collective-permute-start.50 = (bf16[256,768]{1,0:T(8,128)(2,1)S(1)}, bf16[256,768]{1,0:T(8,128)(2,1)S(1)}, u32[]{:S(2)}, u32[]{:S(2)}) collective-permute-start(bf16[256,768]{1,0:T(8,128)(2,1)S(1)} %fusion.22), channel_id=1, source_target_pairs={{0,2},{1,3},{2,0},{3,1},{4,6},{5,7},{6,4},{7,5},{8,10},{9,11},{10,... | collective-permute-start | bytes 1179656 | tf_op jit(solution)/shard_map/ppermute | solution.py:86
  457.9 24.4 %collective-permute-start.46 = (bf16[256,768]{1,0:T(8,128)(2,1)S(1)}, bf16[256,768]{1,0:T(8,128)(2,1)S(1)}, u32[]{:S(2)}, u32[]{:S(2)}) collective-permute-start(bf16[256,768]{1,0:T(8,128)(2,1)S(1)} %fusion.20), channel_id=1, source_target_pairs={{0,2},{1,3},{2,0},{3,1},{4,6},{5,7},{6,4},{7,5},{8,10},{9,11},{10,... | collective-permute-start | bytes 1179656 | tf_op jit(solution)/shard_map/ppermute | solution.py:86
  466.3 24.5 %collective-permute-start.66 = (bf16[4,96,512]{2,1,0:T(8,128)(2,1)S(1)}, bf16[4,96,512]{2,1,0:T(8,128)(2,1)S(1)}, u32[]{:S(2)}, u32[]{:S(2)}) collective-permute-start(bf16[4,96,512]{2,1,0:T(8,128)(2,1)S(1)} %fusion.24), channel_id=1, source_target_pairs={{0,4},{4,0},{8,12},{12,8},{16,20},{20,16},{24,28},{28,24},{1,5},{5... | collective-permute-start | bytes 1179656 | tf_op jit(solution)/shard_map/ppermute | solution.py:86
  504.4 34.7 %collective-permute-start.39 = (bf16[2,3,256,768]{3,2,1,0:T(8,128)(2,1)S(1)}, bf16[2,3,256,768]{3,2,1,0:T(8,128)(2,1)}, u32[]{:S(2)}, u32[]{:S(2)}) collective-permute-start(bf16[2,3,256,768]{3,2,1,0:T(8,128)(2,1)S(1)} %copy-done.13), channel_id=1, source_target_pairs={{0,1},{1,0},{2,3},{3,2},{4,5},{5,4},{6,7},{7,6},{8,9},{9,8},{10,11... | collective-permute-start | bytes 7077896 | tf_op jit(solution)/shard_map/ppermute | solution.py:86
  504.6 26.1 %collective-permute-start.51 = (bf16[256,768]{1,0:T(8,128)(2,1)}, bf16[256,768]{1,0:T(8,128)(2,1)S(1)}, u32[]{:S(2)}, u32[]{:S(2)}) collective-permute-start(bf16[256,768]{1,0:T(8,128)(2,1)} %get-tuple-element.294), channel_id=1, source_target_pairs={{0,2},{1,3},{2,0},{3,1},{4,6},{5,7},{6,4},{7,5},{8,10},{9,11},{10,... | collective-permute-start | bytes 1179656 | tf_op jit(solution)/shard_map/ppermute | solution.py:86
  513.8 19.6 %collective-permute-start.52 = (bf16[256,768]{1,0:T(8,128)(2,1)S(1)}, bf16[256,768]{1,0:T(8,128)(2,1)}, u32[]{:S(2)}, u32[]{:S(2)}) collective-permute-start(bf16[256,768]{1,0:T(8,128)(2,1)S(1)} %copy-done.12), channel_id=1, source_target_pairs={{0,2},{1,3},{2,0},{3,1},{4,6},{5,7},{6,4},{7,5},{8,10},{9,11},{10,... | collective-permute-start | bytes 1179656 | tf_op jit(solution)/shard_map/ppermute | solution.py:86
  520.1 15.3 %collective-permute-start.53 = (bf16[256,768]{1,0:T(8,128)(2,1)S(1)}, bf16[256,768]{1,0:T(8,128)(2,1)S(1)}, u32[]{:S(2)}, u32[]{:S(2)}) collective-permute-start(bf16[256,768]{1,0:T(8,128)(2,1)S(1)} %get-tuple-element.295), channel_id=1, source_target_pairs={{0,2},{1,3},{2,0},{3,1},{4,6},{5,7},{6,4},{7,5},{8,10},{9,11},{10,... | collective-permute-start | bytes 1179656 | tf_op jit(solution)/shard_map/ppermute | solution.py:86
  526.0 26.1 %collective-permute-start.77 = (bf16[2,4,96,768]{3,2,1,0:T(8,128)(2,1)}, bf16[2,4,96,768]{3,2,1,0:T(8,128)(2,1)}, u32[]{:S(2)}, u32[]{:S(2)}) collective-permute-start(bf16[2,4,96,768]{3,2,1,0:T(8,128)(2,1)} %fusion.5), channel_id=1, source_target_pairs={{0,4},{4,0},{8,12},{12,8},{16,20},{20,16},{24,28},{28,24},{1,5},{5... | collective-permute-start | bytes 3538952 | tf_op jit(solution)/shard_map/ppermute | solution.py:86
  530.7 29.2 %collective-permute-start.71 = (bf16[2,4,96,768]{3,2,1,0:T(8,128)(2,1)}, bf16[2,4,96,768]{3,2,1,0:T(8,128)(2,1)}, u32[]{:S(2)}, u32[]{:S(2)}) collective-permute-start(bf16[2,4,96,768]{3,2,1,0:T(8,128)(2,1)} %fusion.4), channel_id=1, source_target_pairs={{0,2},{1,3},{2,0},{3,1},{4,6},{5,7},{6,4},{7,5},{8,10},{9,11},{10,... | collective-permute-start | bytes 3538952 | tf_op jit(solution)/shard_map/ppermute | solution.py:86
  533.4 29.2 %collective-permute-start.54 = (bf16[2,256,768]{2,1,0:T(8,128)(2,1)}, bf16[2,256,768]{2,1,0:T(8,128)(2,1)}, u32[]{:S(2)}, u32[]{:S(2)}) collective-permute-start(bf16[2,256,768]{2,1,0:T(8,128)(2,1)} %pad_maximum_fusion.5), channel_id=1, source_target_pairs={{0,1},{1,0},{2,3},{3,2},{4,5},{5,4},{6,7},{7,6},{8,9},{9,8},{10,11... | collective-permute-start | bytes 2359304 | tf_op jit(solution)/shard_map/ppermute | solution.py:86
  535.4 27.1 %collective-permute-start.55 = (bf16[2,256,768]{2,1,0:T(8,128)(2,1)}, bf16[2,256,768]{2,1,0:T(8,128)(2,1)}, u32[]{:S(2)}, u32[]{:S(2)}) collective-permute-start(bf16[2,256,768]{2,1,0:T(8,128)(2,1)} %pad_maximum_fusion.6), channel_id=1, source_target_pairs={{0,1},{1,0},{2,3},{3,2},{4,5},{5,4},{6,7},{7,6},{8,9},{9,8},{10,11... | collective-permute-start | bytes 2359304 | tf_op jit(solution)/shard_map/ppermute | solution.py:86
  539.1 23.5 %collective-permute-start.56 = (bf16[2,256,768]{2,1,0:T(8,128)(2,1)}, bf16[2,256,768]{2,1,0:T(8,128)(2,1)S(1)}, u32[]{:S(2)}, u32[]{:S(2)}) collective-permute-start(bf16[2,256,768]{2,1,0:T(8,128)(2,1)} %pad_maximum_fusion.7), channel_id=1, source_target_pairs={{0,1},{1,0},{2,3},{3,2},{4,5},{5,4},{6,7},{7,6},{8,9},{9,8},{10,11... | collective-permute-start | bytes 2359304 | tf_op jit(solution)/shard_map/ppermute | solution.py:86
  553.8 23.1 %collective-permute-start.78 = (bf16[4,96,768]{2,1,0:T(8,128)(2,1)S(1)}, bf16[4,96,768]{2,1,0:T(8,128)(2,1)S(1)}, u32[]{:S(2)}, u32[]{:S(2)}) collective-permute-start(bf16[4,96,768]{2,1,0:T(8,128)(2,1)S(1)} %fusion.17), channel_id=1, source_target_pairs={{0,2},{1,3},{2,0},{3,1},{4,6},{5,7},{6,4},{7,5},{8,10},{9,11},{10,... | collective-permute-start | bytes 1769480 | tf_op jit(solution)/shard_map/ppermute | solution.py:86
  561.6 19.9 %collective-permute-start.72 = (bf16[4,96,768]{2,1,0:T(8,128)(2,1)S(1)}, bf16[4,96,768]{2,1,0:T(8,128)(2,1)S(1)}, u32[]{:S(2)}, u32[]{:S(2)}) collective-permute-start(bf16[4,96,768]{2,1,0:T(8,128)(2,1)S(1)} %fusion.16), channel_id=1, source_target_pairs={{0,4},{4,0},{8,12},{12,8},{16,20},{20,16},{24,28},{28,24},{1,5},{5... | collective-permute-start | bytes 1769480 | tf_op jit(solution)/shard_map/ppermute | solution.py:86
  582.3 19.5 %collective-permute-start.74 = (bf16[96,768]{1,0:T(8,128)(2,1)S(1)}, bf16[96,768]{1,0:T(8,128)(2,1)S(1)}, u32[]{:S(2)}, u32[]{:S(2)}) collective-permute-start(bf16[96,768]{1,0:T(8,128)(2,1)S(1)} %get-tuple-element.308), channel_id=1, source_target_pairs={{0,16},{4,20},{8,24},{12,28},{16,0},{20,4},{24,8},{28,12},{1,17},{... | collective-permute-start | bytes 442376 | tf_op jit(solution)/shard_map/ppermute | solution.py:86
  587.1 14.7 %collective-permute-start.75 = (bf16[96,768]{1,0:T(8,128)(2,1)S(1)}, bf16[96,768]{1,0:T(8,128)(2,1)S(1)}, u32[]{:S(2)}, u32[]{:S(2)}) collective-permute-start(bf16[96,768]{1,0:T(8,128)(2,1)S(1)} %get-tuple-element.307), channel_id=1, source_target_pairs={{0,24},{4,28},{8,16},{12,20},{16,8},{20,12},{24,0},{28,4},{1,25},{... | collective-permute-start | bytes 442376 | tf_op jit(solution)/shard_map/ppermute | solution.py:86
  (122 other events, 1196.4 us)
